TPU v7x, 128 devices: a whole 4x4x4 slice. The times are simulated.
128 devices in a mesh: row: 8 (over x_hi, z), col: 8 (over y, core), fsdp: 2 (over x_lo).
Axes of the slice: x: 4 (x_hi: 2, x_lo: 2; x = x_hi * 2 + x_lo), y: 4, z: 4, core: 2. Of those that a mesh axis runs over, the one named last changes fastest.
Arguments:
- delta_one: float32 [8, 8, 1024, 2048], P('row', 'col', 'fsdp'), may hold values from -6 to 6
- delta_two: float32 [8, 8, 1024, 2048], P('row', 'col', 'fsdp'), may hold values from -6 to 6
- params_one: float32 [8, 1024, 2048], P('row', 'fsdp', 'col'), may hold values from -6 to 6
- moment_one: float32 [8, 1024, 2048], P('row', 'fsdp', 'col'), may hold values from -6 to 6
- params_two: float32 [8, 1024, 2048], P('col', 'fsdp', 'row'), may hold values from -6 to 6
- moment_two: float32 [8, 1024, 2048], P('col', 'fsdp', 'row'), may hold values from -6 to 6
Outputs:
- new_params_one: float32 [8, 1024, 2048], P('row', 'fsdp', 'col')
- new_moment_one: float32 [8, 1024, 2048], P('row', 'fsdp', 'col')
- copy_one: bfloat16 [8, 1024, 2048], P('row', 'fsdp')
- new_params_two: float32 [8, 1024, 2048], P('col', 'fsdp', 'row')
- new_moment_two: float32 [8, 1024, 2048], P('col', 'fsdp', 'row')
- copy_two: bfloat16 [8, 1024, 2048], P('col', 'fsdp')
All inputs are finite; a program needn't handle non-finite values.
Results may differ from a plain program's by a relative error of at most 0.001.
Values may be sent and summed in bfloat16 or wider, within the bound.
A program may use at most 128 MiB of HBM per device.

v0:
```python
import jax
import jax.numpy as jnp
from jax import lax
from jax.sharding import PartitionSpec as P


def nesterov(grad, params, moment):
    moment_next = 0.9 * moment + grad
    params_next = params - 0.7 * (grad + 0.9 * moment_next)
    return (params_next, moment_next)


def body(delta_one, delta_two, params_one, moment_one, params_two, moment_two):
    col_count = lax.axis_size("col")
    row_count = lax.axis_size("row")
    grad_one = lax.psum(delta_one, "col")[:, 0] / col_count
    grad_two = lax.psum(delta_two, "row")[0] / row_count
    full_params_one, full_moment_one = (
        lax.all_gather(params_one, "col", axis=2, tiled=True),
        lax.all_gather(moment_one, "col", axis=2, tiled=True),
    )
    full_params_two, full_moment_two = (
        lax.all_gather(params_two, "row", axis=2, tiled=True),
        lax.all_gather(moment_two, "row", axis=2, tiled=True),
    )
    whole_params_one, whole_moment_one = nesterov(grad_one, full_params_one, full_moment_one)
    whole_params_two, whole_moment_two = nesterov(grad_two, full_params_two, full_moment_two)
    width_one = params_one.shape[2]
    width_two = params_two.shape[2]
    start_one = lax.axis_index("col") * width_one
    start_two = lax.axis_index("row") * width_two
    first_params = lax.dynamic_slice_in_dim(whole_params_one, start_one, width_one, 2)
    first_moment = lax.dynamic_slice_in_dim(whole_moment_one, start_one, width_one, 2)
    second_params = lax.dynamic_slice_in_dim(whole_params_two, start_two, width_two, 2)
    second_moment = lax.dynamic_slice_in_dim(whole_moment_two, start_two, width_two, 2)
    first_copy = whole_params_one.astype(jnp.bfloat16)
    second_copy = whole_params_two.astype(jnp.bfloat16)
    return (first_params, first_moment, first_copy, second_params, second_moment, second_copy)


def solution(mesh):
    placed = (
        P("row", "col", "fsdp", None),
        P("row", "col", "fsdp", None),
        P("row", "fsdp", "col"),
        P("row", "fsdp", "col"),
        P("col", "fsdp", "row"),
        P("col", "fsdp", "row"),
    )
    return jax.shard_map(
        body,
        mesh=mesh,
        in_specs=placed,
        out_specs=(
            P("row", "fsdp", "col"),
            P("row", "fsdp", "col"),
            P("row", "fsdp", None),
            P("col", "fsdp", "row"),
            P("col", "fsdp", "row"),
            P("col", "fsdp", None),
        ),
        check_vma=False,
    )
```

profile of v0, /device:TPU:1, one launch (start us, length us, event | category | flops | bytes accessed | tf_op | source)
XLA Modules:
  0.0 429.4 jit_solution(7278530664041322082)
XLA Ops:
  7.2 0.0 all-reduce.3.cloned.1.call-start
  7.2 0.7 all-reduce.3.cloned.1.call-update
  7.9 0.0 all-gather.5.cloned.1.call-start
  7.9 0.7 all-gather.5.cloned.1.call-update
  8.6 0.0 all-gather.7.cloned.1.call-start
  8.7 0.7 all-gather.7.cloned.1.call-update
  9.4 0.0 all-reduce.5.cloned.1.call-start
  9.4 0.5 all-reduce.5.cloned.1.call-update
  10.0 0.0 all-gather.9.cloned.1.call-start
  10.0 0.5 all-gather.9.cloned.1.call-update
  10.5 0.0 all-gather.11.cloned.1.call-start
  10.6 0.5 all-gather.11.cloned.1.call-update
  11.1 73.2 %all-reduce.3.cloned.1.call-done = f32[1,1,512,2048]{3,2,1,0:T(8,128)} async-done(((f32[1,1,512,2048]{3,2,1,0:T(8,128)}), f32[1,1,512,2048]{3,2,1,0:T(8,128)}) %all-reduce.3.cloned.1.call-update) | async-done | bytes 4194320 | tf_op jit(solution)/shard_map/psum | solution.py:16
  84.4 36.1 %all-gather.5.cloned.1.call-done = f32[1,512,2048]{2,1,0:T(8,128)} async-done(((f32[1,512,256]{2,1,0:T(8,128)}), f32[1,512,2048]{2,1,0:T(8,128)}) %all-gather.5.cloned.1.call-update) | async-done | bytes 4194320 | tf_op jit(solution)/shard_map/all_gather | solution.py:19
  120.4 33.8 %all-gather.7.cloned.1.call-done = f32[1,512,2048]{2,1,0:T(8,128)} async-done(((f32[1,512,256]{2,1,0:T(8,128)}), f32[1,512,2048]{2,1,0:T(8,128)}) %all-gather.7.cloned.1.call-update) | async-done | bytes 4194320 | tf_op jit(solution)/shard_map/all_gather | solution.py:20
  154.2 7.6 %fusion.6 = (bf16[1,512,2048]{2,1,0:T(8,128)(2,1)}, f32[1,512,2048]{2,1,0:T(8,128)S(1)}, f32[1,512,2048]{2,1,0:T(8,128)S(1)}) fusion(f32[1,512,2048]{2,1,0:T(8,128)} %all-gather.5.cloned.1.call-done, f32[1,512,2048]{2,1,0:T(8,128)} %all-gather.7.cloned.1.call-done, f32[1,1,512,2048]{3,2,1,0:T(8,128)} %all-reduce.3.cloned.1.call-done), kind=kLoop, calls=%fused_computation.13 | loop fusion | flops 8388608 | bytes 23068672 | tf_op jit(solution)/shard_map/convert_element_type | solution.py:36
  161.8 1.1 constant_dynamic-slice_fusion.2
  162.8 103.3 %all-reduce.5.cloned.1.call-done = f32[1,1,512,2048]{3,2,1,0:T(8,128)} async-done(((f32[1,1,512,2048]{3,2,1,0:T(8,128)}), f32[1,1,512,2048]{3,2,1,0:T(8,128)}) %all-reduce.5.cloned.1.call-update) | async-done | bytes 4194320 | tf_op jit(solution)/shard_map/psum | solution.py:17
  266.2 74.0 %all-gather.9.cloned.1.call-done = f32[1,512,2048]{2,1,0:T(8,128)} async-done(((f32[1,512,256]{2,1,0:T(8,128)}), f32[1,512,2048]{2,1,0:T(8,128)}) %all-gather.9.cloned.1.call-update) | async-done | bytes 4194320 | tf_op jit(solution)/shard_map/all_gather | solution.py:23
  340.2 73.7 %all-gather.11.cloned.1.call-done = f32[1,512,2048]{2,1,0:T(8,128)} async-done(((f32[1,512,256]{2,1,0:T(8,128)}), f32[1,512,2048]{2,1,0:T(8,128)}) %all-gather.11.cloned.1.call-update) | async-done | bytes 4194320 | tf_op jit(solution)/shard_map/all_gather | solution.py:24
  413.9 7.6 %fusion.4 = (bf16[1,512,2048]{2,1,0:T(8,128)(2,1)}, f32[1,512,2048]{2,1,0:T(8,128)S(1)}, f32[1,512,2048]{2,1,0:T(8,128)S(1)}) fusion(f32[1,512,2048]{2,1,0:T(8,128)} %all-gather.9.cloned.1.call-done, f32[1,512,2048]{2,1,0:T(8,128)} %all-gather.11.cloned.1.call-done, f32[1,1,512,2048]{3,2,1,0:T(8,128)} %all-reduce.5.cloned.1.call-done), kind=kLoop, calls=%fused_computation.12 | loop fusion | flops 8388608 | bytes 23068672 | tf_op jit(solution)/shard_map/convert_element_type | solution.py:37
  421.5 1.1 constant_dynamic-slice_fusion
Async XLA Ops:
  7.2 77.2 %all-reduce.3.cloned.1.call-start = ((), (), s32[]{:S(2)}) async-start(), calls=%async_computation.1 | async-start | bytes 8388608 | tf_op jit(solution)/shard_map/psum | solution.py:16
  7.9 112.5 %all-gather.5.cloned.1.call-start = ((), (), s32[]{:S(2)}) async-start(), calls=%async_computation | async-start | bytes 4718592 | tf_op jit(solution)/shard_map/all_gather | solution.py:19
  8.6 145.6 %all-gather.7.cloned.1.call-start = ((), (), s32[]{:S(2)}) async-start(), calls=%async_computation.2 | async-start | bytes 4718592 | tf_op jit(solution)/shard_map/all_gather | solution.py:20
  9.4 256.8 %all-reduce.5.cloned.1.call-start = ((), (), s32[]{:S(2)}) async-start(), calls=%async_computation.4 | async-start | bytes 8388608 | tf_op jit(solution)/shard_map/psum | solution.py:17
  10.0 330.3 %all-gather.9.cloned.1.call-start = ((), (), s32[]{:S(2)}) async-start(), calls=%async_computation.3 | async-start | bytes 4718592 | tf_op jit(solution)/shard_map/all_gather | solution.py:23
  10.5 403.4 %all-gather.11.cloned.1.call-start = ((), (), s32[]{:S(2)}) async-start(), calls=%async_computation.5 | async-start | bytes 4718592 | tf_op jit(solution)/shard_map/all_gather | solution.py:24
Sparse Core Ops, SparseCore 0:
  10.4 73.9 all-reduce.2
  86.0 34.3 all-gather.4
  122.1 32.0 all-gather.6
  156.6 109.5 all-reduce.4
  268.2 71.9 all-gather.8
  342.2 71.6 all-gather.10
where the time goes:
time: 430 us; the launch traced here: 429 us
  waiting for transfers between devices  398 us (93%)
  other arithmetic  15.1 us (4%)
  between operations  14.1 us (3%)
    psum x1, waiting for transfers between devices, body(): grad_two = lax.psum(delta_two, 'row')[0] / row_count  103 us
    all_gather x1, waiting for transfers between devices, body(): lax.all_gather(params_two, 'row', axis=2, tiled=True)  74 us
    all_gather x1, waiting for transfers between devices, body(): lax.all_gather(moment_two, 'row', axis=2, tiled=True)  73.7 us
    psum x1, waiting for transfers between devices, body(): grad_one = lax.psum(delta_one, 'col')[:, 0] / col_count  73.2 us
    all_gather x1, waiting for transfers between devices, body(): lax.all_gather(params_one, 'col', axis=2, tiled=True)  36.1 us
    all_gather x1, waiting for transfers between devices, body(): lax.all_gather(moment_one, 'col', axis=2, tiled=True)  33.8 us
  transfers between devices with their start and end apart: 6, of which 6 were waited for; matrix products, arithmetic and copies ran while one was open for 2% of the time, Pallas kernels for 0%

commit v1 on v0

v1 whole, which is shorter than its diff:
```python
import jax
import jax.numpy as jnp
from jax import lax
from jax.experimental import pallas as pl
from jax.experimental.pallas import tpu as pltpu
from jax.sharding import PartitionSpec as P

MESH = pl.DeviceIdType.MESH
ROWS, WIDTH = 512, 256
STEP = 16
PIECES_TWO = ((0, 0, 96), (1, 96, 96), (2, 192, 80), (0, 272, 80), (1, 352, 80), (2, 432, 80))
PIECES_ONE = ((0, 0, 128), (1, 128, 128), (0, 256, 128), (1, 384, 128))
N_COPIES = 14 * (len(PIECES_TWO) + len(PIECES_ONE))


def code(x, power):
    t = x * (2.0**power)
    t2 = t * t
    return ((t2 * t2) * t2 * (t * jnp.abs(t))).astype(jnp.bfloat16)


def decode(y, power):
    y = y.astype(jnp.float32)
    quarter = lax.rsqrt(lax.rsqrt(jnp.maximum(jnp.abs(y), 2.0**-126)))
    sign = jnp.where(y < 0, -(2.0**-power), 2.0**-power)
    return quarter * lax.rsqrt(quarter) * sign


def kernel(
    d1, d2, p1, m1, p2, m2,
    np1, nm1, c1, np2, nm2, c2,
    d1v, d2v, pm, pmo, cv1, cv2,
    s2a, s2b, s2c, r2a, r2b, r2c,
    s1b, s1c, r1a, r1b, r1c,
    send_sem, recv_sem, load_sem, store_sem,
):
    row, col, fsdp = lax.axis_index("row"), lax.axis_index("col"), lax.axis_index("fsdp")
    xh, z = row // 4, row % 4
    y, core = col // 2, col % 2

    def flip4(v, mask):
        if mask == 0:
            return v
        if mask == 1:
            return v + 1 - 2 * (v % 2)
        if mask == 3:
            return 3 - v
        return 2 - v + 2 * (v % 2)

    def row_of(mask):
        high = 1 - xh if mask & 4 else xh
        return high * 4 + flip4(z, mask & 3)

    def col_of(mask):
        low = 1 - core if mask & 1 else core
        return flip4(y, mask >> 1) * 2 + low

    def device_two(mask):
        return (row_of(mask), col, fsdp)

    def device_one(mask):
        return (row, col_of(mask), fsdp)

    orders_two = ((1, 3, 4), (3, 4, 1), (4, 1, 3))
    orders_one = ((1, 2, 6), (1, 6, 2))

    def cols(index):
        return pl.ds(pl.multiple_of(index * WIDTH, WIDTH), WIDTH)

    n_sent = [0]
    sent = []

    def send(src, dst, device):
        i = n_sent[0]
        n_sent[0] += 1
        copy = pltpu.make_async_remote_copy(
            src_ref=src, dst_ref=dst, send_sem=send_sem.at[i], recv_sem=recv_sem.at[i],
            device_id=device, device_id_type=MESH,
        )
        copy.start()
        sent.append(copy)
        return copy

    loads, stores = [], []

    def load(src, dst):
        copy = pltpu.make_async_copy(src, dst, load_sem.at[len(loads)])
        copy.start()
        loads.append(copy)
        return copy

    def store(src, dst):
        copy = pltpu.make_async_copy(src, dst, store_sem.at[len(stores)])
        copy.start()
        stores.append(copy)
        return copy

    loaded_two, loaded_one = {}, {}
    for k, (o, r0, n) in enumerate(PIECES_TWO):
        loaded_two[k] = load(d2.at[pl.ds(r0, n)], d2v.at[pl.ds(r0, n)])
    for k, (o, r0, n) in enumerate(PIECES_ONE):
        loaded_one[k] = load(d1.at[pl.ds(r0, n)], d1v.at[pl.ds(r0, n)])
    loaded_pm = [load(ref, pm.at[i]) for i, ref in enumerate((p1, m1, p2, m2))]

    barrier = pltpu.get_barrier_semaphore()
    for mask in (1, 3, 4):
        pl.semaphore_signal(barrier, inc=1, device_id=device_two(mask), device_id_type=MESH)
    for mask in (1, 2, 6):
        pl.semaphore_signal(barrier, inc=1, device_id=device_one(mask), device_id_type=MESH)
    pl.semaphore_wait(barrier, 6)

    def over(r0, n, body):
        def step(i, carry):
            body(pl.ds(pl.multiple_of(r0 + i * STEP, STEP), STEP))
            return carry

        lax.fori_loop(0, n // STEP, step, 0)

    def block_mask(order, e):
        mask = 0
        for bit, m in zip((4, 2, 1), order):
            if e & bit:
                mask ^= m
        return mask

    class Level:
        def __init__(self, pieces, orders, index_of, device, dv, cv, loaded, param, out, copy_out):
            self.pieces, self.orders, self.index_of, self.device = pieces, orders, index_of, device
            self.dv, self.cv, self.loaded = dv, cv, loaded
            self.param, self.out, self.copy_out = param, out, copy_out
            self.got = {}

        def at(self, k):
            o, r0, n = self.pieces[k]
            return self.orders[o], r0, n, pl.ds(r0, n)

        def cols(self, order, e):
            return cols(self.index_of(block_mask(order, e)))

        def give(self, k, e, stage):
            order, r0, n, rs = self.at(k)
            part = self.cv.at[rs, self.cols(order, e)]
            bit = (4, 2, 1)[stage]
            self.got[k, e ^ bit] = send(part, part, self.device(order[stage]))

        def finish(self, k, grad_of):
            order, r0, n, rs = self.at(k)
            mine = self.cols(order, 0)
            i = self.param

            def body(s):
                grad = grad_of(s) * 0.125
                moment = 0.9 * pm[i + 1, s] + grad
                params = pm[i, s] - 0.7 * (grad + 0.9 * moment)
                pmo[i + 1, s] = moment
                pmo[i, s] = params
                self.cv[s, mine] = params.astype(jnp.bfloat16)

            over(r0, n, body)
            self.give(k, 0, 2)
            self.give(k, 0, 1)
            self.give(k, 0, 0)
            store(pmo.at[i, rs], self.out[0].at[rs])
            store(pmo.at[i + 1, rs], self.out[1].at[rs])

        def gather_a(self, k):
            self.got[k, 1].wait_recv()
            self.give(k, 1, 1)
            self.give(k, 1, 0)

        def gather_b(self, k):
            self.got[k, 2].wait_recv()
            self.give(k, 2, 0)
            self.got[k, 3].wait_recv()
            self.give(k, 3, 0)

        def gather_c(self, k):
            order, r0, n, rs = self.at(k)
            for e in (4, 5, 6, 7):
                self.got[k, e].wait_recv()
            store(self.cv.at[rs], self.copy_out.at[rs])

    two = Level(PIECES_TWO, orders_two, row_of, device_two, d2v, cv2, loaded_two, 2, (np2, nm2), c2)
    one = Level(PIECES_ONE, orders_one, col_of, device_one, d1v, cv1, loaded_one, 0, (np1, nm1), c1)
    red = {}

    def two_a(k):
        order, r0, n, rs = two.at(k)
        loaded_two[k].wait()
        for q_pair in ((3, 2), (1, 0)):
            places = [(q, two.cols(order, 4 + q)) for q in q_pair]

            def body(s):
                for q, c in places:
                    s2a[q, s] = code(d2v[s, c], 13)

            over(r0, n, body)
            for q in q_pair:
                red["2a", k, q] = send(s2a.at[q, rs], r2a.at[q, rs], two.device(order[0]))

    def two_b(k):
        order, r0, n, rs = two.at(k)
        red["2a", k, 3].wait_recv()
        red["2a", k, 2].wait_recv()
        places = [(q, two.cols(order, 2 + q)) for q in (1, 0)]

        def body(s):
            for q, c in places:
                s2b[q, s] = code(d2v[s, c] + decode(r2a[2 + q, s], 13), 12)

        over(r0, n, body)
        for q in (1, 0):
            red["2b", k, q] = send(s2b.at[q, rs], r2b.at[q, rs], two.device(order[1]))

    def two_c(k):
        order, r0, n, rs = two.at(k)
        red["2a", k, 1].wait_recv()
        red["2b", k, 1].wait_recv()
        c = two.cols(order, 1)

        def body(s):
            s2c[s] = code(d2v[s, c] + decode(r2a[1, s], 13) + decode(r2b[1, s], 12), 11)

        over(r0, n, body)
        red["2c", k] = send(s2c.at[rs], r2c.at[rs], two.device(order[2]))

    def two_d(k):
        order, r0, n, rs = two.at(k)
        red["2a", k, 0].wait_recv()
        red["2b", k, 0].wait_recv()
        red["2c", k].wait_recv()
        c = two.cols(order, 0)
        two.finish(k, lambda s: d2v[s, c] + decode(r2a[0, s], 13) + decode(r2b[0, s], 12) + decode(r2c[s], 11))

    def one_a(k):
        order, r0, n, rs = one.at(k)
        for q in (3, 2, 1, 0):
            red["1a", k, q] = send(d1.at[rs, one.cols(order, 4 + q)], r1a.at[q, rs], one.device(order[0]))

    def one_b(k):
        order, r0, n, rs = one.at(k)
        loaded_one[k].wait()
        red["1a", k, 3].wait_recv()
        red["1a", k, 2].wait_recv()
        places = [(q, one.cols(order, 2 + q)) for q in (1, 0)]

        def body(s):
            for q, c in places:
                s1b[q, s] = d1v[s, c] + r1a[2 + q, s]

        over(r0, n, body)
        for q in (1, 0):
            red["1b", k, q] = send(s1b.at[q, rs], r1b.at[q, rs], one.device(order[1]))

    def one_c(k):
        order, r0, n, rs = one.at(k)
        red["1a", k, 1].wait_recv()
        red["1b", k, 1].wait_recv()
        c = one.cols(order, 1)

        def body(s):
            s1c[s] = d1v[s, c] + r1a[1, s] + r1b[1, s]

        over(r0, n, body)
        red["1c", k] = send(s1c.at[rs], r1c.at[rs], one.device(order[2]))

    def one_d(k):
        order, r0, n, rs = one.at(k)
        red["1a", k, 0].wait_recv()
        red["1b", k, 0].wait_recv()
        red["1c", k].wait_recv()
        c = one.cols(order, 0)
        one.finish(k, lambda s: d1v[s, c] + r1a[0, s] + r1b[0, s] + r1c[s])

    for k in range(4):
        one_a(k)
    for k in range(3):
        two_a(k)
    for k in range(2):
        one_b(k)
    for k in range(3, 6):
        two_a(k)
    for k in range(2, 4):
        one_b(k)
    for k in range(3):
        two_b(k)
    for k in range(3, 6):
        two_b(k)
    for k in range(3):
        two_c(k)
    for k in range(2):
        one_c(k)
    for k in range(3, 6):
        two_c(k)
    for copy in loaded_pm:
        copy.wait()
    for k in range(3):
        two_d(k)
    for k in range(2, 4):
        one_c(k)
    for k in range(3, 6):
        two_d(k)
    for k in range(3):
        two.gather_a(k)
    for k in range(2):
        one_d(k)
    for k in range(3, 6):
        two.gather_a(k)
    for k in range(3):
        two.gather_b(k)
    for k in range(2, 4):
        one_d(k)
    for k in range(2):
        one.gather_a(k)
    for k in range(3, 6):
        two.gather_b(k)
    for k in range(2):
        one.gather_b(k)
    for k in range(2, 4):
        one.gather_a(k)
    for k in range(3):
        two.gather_c(k)
    for k in range(2, 4):
        one.gather_b(k)
    for k in range(2):
        one.gather_c(k)
    for k in range(3, 6):
        two.gather_c(k)
    for k in range(2, 4):
        one.gather_c(k)
    for copy in sent:
        copy.wait_send()
    for copy in stores:
        copy.wait()
    assert n_sent[0] == N_COPIES


def body(delta_one, delta_two, params_one, moment_one, params_two, moment_two):
    hbm = pl.BlockSpec(memory_space=pl.ANY)
    small = jax.ShapeDtypeStruct((ROWS, WIDTH), jnp.float32)
    wide = jax.ShapeDtypeStruct((ROWS, 8 * WIDTH), jnp.bfloat16)
    f32, bf16 = jnp.float32, jnp.bfloat16
    n_local = len(PIECES_TWO) + len(PIECES_ONE)
    outs = pl.pallas_call(
        kernel,
        out_shape=(small, small, wide, small, small, wide),
        in_specs=[hbm] * 6,
        out_specs=[hbm] * 6,
        scratch_shapes=[
            pltpu.VMEM((ROWS, 8 * WIDTH), f32),
            pltpu.VMEM((ROWS, 8 * WIDTH), f32),
            pltpu.VMEM((4, ROWS, WIDTH), f32),
            pltpu.VMEM((4, ROWS, WIDTH), f32),
            pltpu.VMEM((ROWS, 8 * WIDTH), bf16),
            pltpu.VMEM((ROWS, 8 * WIDTH), bf16),
            pltpu.VMEM((4, ROWS, WIDTH), bf16),
            pltpu.VMEM((2, ROWS, WIDTH), bf16),
            pltpu.VMEM((ROWS, WIDTH), bf16),
            pltpu.VMEM((4, ROWS, WIDTH), bf16),
            pltpu.VMEM((2, ROWS, WIDTH), bf16),
            pltpu.VMEM((ROWS, WIDTH), bf16),
            pltpu.VMEM((2, ROWS, WIDTH), f32),
            pltpu.VMEM((ROWS, WIDTH), f32),
            pltpu.VMEM((4, ROWS, WIDTH), f32),
            pltpu.VMEM((2, ROWS, WIDTH), f32),
            pltpu.VMEM((ROWS, WIDTH), f32),
            pltpu.SemaphoreType.DMA((N_COPIES,)),
            pltpu.SemaphoreType.DMA((N_COPIES,)),
            pltpu.SemaphoreType.DMA((n_local + 4,)),
            pltpu.SemaphoreType.DMA((3 * n_local,)),
        ],
        compiler_params=pltpu.CompilerParams(
            collective_id=0, has_side_effects=True, vmem_limit_bytes=48 * 1024 * 1024
        ),
        name="outer_step",
    )(delta_one[0, 0], delta_two[0, 0], params_one[0], moment_one[0], params_two[0], moment_two[0])
    return tuple(out[None] for out in outs)


def solution(mesh):
    placed = (
        P("row", "col", "fsdp", None),
        P("row", "col", "fsdp", None),
        P("row", "fsdp", "col"),
        P("row", "fsdp", "col"),
        P("col", "fsdp", "row"),
        P("col", "fsdp", "row"),
    )
    return jax.shard_map(
        body,
        mesh=mesh,
        in_specs=placed,
        out_specs=(
            P("row", "fsdp", "col"),
            P("row", "fsdp", "col"),
            P("row", "fsdp", None),
            P("col", "fsdp", "row"),
            P("col", "fsdp", "row"),
            P("col", "fsdp", None),
        ),
        check_vma=False,
    )
```

time: 430 us -> 59.5 us (0.14)
  waiting for transfers between devices: 398 us -> 0 us
  Pallas kernels: 0 us -> 48.3 us
  other arithmetic: 15.1 us -> 0 us
  between operations: 14.1 us -> 0.67 us
  local copies, waits for them, and re-layouts: 2.15 us -> 10.2 us
    all_gather x4 -> x0, waiting for transfers between devices: 218 us -> none  [the longest x1 74 us: body(): lax.all_gather(params_two, 'row', axis=2, tiled=True)]
    psum x2 -> x0, waiting for transfers between devices: 177 us -> none  [the longest x1 103 us: body(): grad_two = lax.psum(delta_two, 'row')[0] / row_count]
    pallas_call x0 -> x1, Pallas kernels: none -> 48.3 us  [body(): pl.pallas_call(kernel, out_shape=(small, small, wide, small, small, wide)...]
    convert_element_type x2 -> x0, other arithmetic: 15.1 us -> none  [the longest x1 7.56 us: body(): first_copy = whole_params_one.astype(jnp.bfloat16)]
    unnamed x0 -> x18, local copies, waits for them, and re-layouts: none -> 10.2 us
  transfers between devices with their start and end apart: 6 -> 0, of which waited for: 6 -> 0; matrix products, arithmetic and copies ran while one was open for 2% -> 0% of each run, Pallas kernels for 0% -> 0%
where the time goes in v1:
time: 59.5 us; the launch traced here: 59.1 us
  Pallas kernels  48.3 us (81%)
  local copies, waits for them, and re-layouts  10.2 us (17%)
  between operations  0.67 us (1%)
    pallas_call x1, Pallas kernels, body(): pl.pallas_call(kernel, out_shape=(small, small, wide, small, small, wide)...  48.3 us
    unnamed x18, local copies, waits for them, and re-layouts  10.2 us

profile of v1, /device:TPU:1, one launch (start us, length us, event | category | flops | bytes accessed | tf_op | source)
XLA Modules:
  0.0 59.1 jit_solution(8309380461235310308)
XLA Ops:
  0.6 0.0 copy-start
  0.6 1.0 %copy-done = f32[1,512,256]{2,1,0:T(8,128)S(1)} copy-done((f32[1,512,256]{2,1,0:T(8,128)S(1)}, f32[1,512,256]{2,1,0:T(8,128)}, u32[]{:S(2)}) %copy-start) | copy-done | bytes 524312
  1.7 0.0 copy-start.1
  1.7 1.0 %copy-done.1 = f32[1,512,256]{2,1,0:T(8,128)S(1)} copy-done((f32[1,512,256]{2,1,0:T(8,128)S(1)}, f32[1,512,256]{2,1,0:T(8,128)}, u32[]{:S(2)}) %copy-start.1) | copy-done | bytes 524312
  2.7 0.0 copy-start.2
  2.7 1.0 %copy-done.2 = f32[1,512,256]{2,1,0:T(8,128)S(1)} copy-done((f32[1,512,256]{2,1,0:T(8,128)S(1)}, f32[1,512,256]{2,1,0:T(8,128)}, u32[]{:S(2)}) %copy-start.2) | copy-done | bytes 524312
  3.8 0.0 copy-start.3
  3.8 1.0 %copy-done.3 = f32[1,512,256]{2,1,0:T(8,128)S(1)} copy-done((f32[1,512,256]{2,1,0:T(8,128)S(1)}, f32[1,512,256]{2,1,0:T(8,128)}, u32[]{:S(2)}) %copy-start.3) | copy-done | bytes 524312
  4.8 48.3 %outer_step.1 = (f32[512,256]{1,0:T(8,128)S(1)}, f32[512,256]{1,0:T(8,128)S(1)}, bf16[512,2048]{1,0:T(8,128)(2,1)}, f32[512,256]{1,0:T(8,128)S(1)}, f32[512,256]{1,0:T(8,128)S(1)}, /*index=5*/bf16[512,2048]{1,0:T(8,128)(2,1)}) custom-call(f32[512,2048]{1,0:T(8,128)} %bitcast.20, f32[512,2048]{1,0:T(8,128)} %bitcast.21, f32[512,256]{1,0:T(8,128)S(1)} %bitcast.12, ...), custom_call_target="tpu_custom_call" | custom-call | tf_op jit(solution)/shard_map/outer_step/pallas_call | solution.py:344
  53.1 0.0 copy-start.5
  53.1 0.8 %copy.18 = f32[1,512,256]{2,1,0:T(8,128)} copy(f32[1,512,256]{2,1,0:T(8,128)S(1)} %bitcast.19) | data formatting | bytes 1048576
  53.9 0.8 %copy.19 = f32[1,512,256]{2,1,0:T(8,128)} copy(f32[1,512,256]{2,1,0:T(8,128)S(1)} %bitcast.18) | data formatting | bytes 1048576
  54.7 0.2 copy-done.5
  54.9 0.0 copy-start.4
  54.9 1.3 %copy.20 = bf16[1,512,2048]{2,1,0:T(8,128)(2,1)} copy(bf16[1,512,2048]{2,1,0:T(8,128)(2,1)S(1)} %bitcast.23) | data formatting | bytes 4194304
  56.2 0.8 %copy.21 = f32[1,512,256]{2,1,0:T(8,128)} copy(f32[1,512,256]{2,1,0:T(8,128)S(1)} %bitcast.17) | data formatting | bytes 1048576
  57.0 0.8 %copy.22 = f32[1,512,256]{2,1,0:T(8,128)} copy(f32[1,512,256]{2,1,0:T(8,128)S(1)} %bitcast.16) | data formatting | bytes 1048576
  57.8 0.0 copy-done.4
  57.8 1.3 %copy.23 = bf16[1,512,2048]{2,1,0:T(8,128)(2,1)} copy(bf16[1,512,2048]{2,1,0:T(8,128)(2,1)S(1)} %bitcast.22) | data formatting | bytes 4194304
Async XLA Ops:
  0.6 1.0 %copy-start = (f32[1,512,256]{2,1,0:T(8,128)S(1)}, f32[1,512,256]{2,1,0:T(8,128)}, u32[]{:S(2)}) copy-start(f32[1,512,256]{2,1,0:T(8,128)} %param.8) | copy-start | bytes 1572868
  1.7 1.0 %copy-start.1 = (f32[1,512,256]{2,1,0:T(8,128)S(1)}, f32[1,512,256]{2,1,0:T(8,128)}, u32[]{:S(2)}) copy-start(f32[1,512,256]{2,1,0:T(8,128)} %param.9) | copy-start | bytes 1572868
  2.7 1.0 %copy-start.2 = (f32[1,512,256]{2,1,0:T(8,128)S(1)}, f32[1,512,256]{2,1,0:T(8,128)}, u32[]{:S(2)}) copy-start(f32[1,512,256]{2,1,0:T(8,128)} %param.10) | copy-start | bytes 1572868
  3.8 1.0 %copy-start.3 = (f32[1,512,256]{2,1,0:T(8,128)S(1)}, f32[1,512,256]{2,1,0:T(8,128)}, u32[]{:S(2)}) copy-start(f32[1,512,256]{2,1,0:T(8,128)} %param.11) | copy-start | bytes 1572868
  53.1 1.8 %copy-start.5 = (bf16[512,2048]{1,0:T(8,128)(2,1)S(1)}, bf16[512,2048]{1,0:T(8,128)(2,1)}, u32[]{:S(2)}) copy-start(bf16[512,2048]{1,0:T(8,128)(2,1)} %get-tuple-element.14) | copy-start | bytes 6291460
  54.9 2.9 %copy-start.4 = (bf16[512,2048]{1,0:T(8,128)(2,1)S(1)}, bf16[512,2048]{1,0:T(8,128)(2,1)}, u32[]{:S(2)}) copy-start(bf16[512,2048]{1,0:T(8,128)(2,1)} %get-tuple-element.17) | copy-start | bytes 6291460

commit v2 on v0

v2 whole, which is shorter than its diff:
```python
import jax
import jax.numpy as jnp
from jax import lax
from jax.experimental import pallas as pl
from jax.experimental.pallas import tpu as pltpu
from jax.sharding import PartitionSpec as P

MESH = pl.DeviceIdType.MESH
ROWS, WIDTH = 512, 256
STEP = 16
PIECES_TWO = ((0, 0, 96), (1, 96, 96), (2, 192, 80), (0, 272, 80), (1, 352, 80), (2, 432, 80))
PIECES_ONE = ((0, 0, 128), (1, 128, 128), (0, 256, 128), (1, 384, 128))
PLAN = (
    (2, "a", 0), (2, "a", 1), (2, "a", 2), (2, "a", 3), (2, "a", 4), (2, "a", 5),
    (1, "a", 0), (1, "a", 1), (1, "a", 2), (1, "a", 3), (2, "b", 0), (2, "b", 1),
    (2, "b", 2), (1, "b", 0), (1, "b", 1), (1, "b", 2), (2, "b", 3), (1, "b", 3),
    (1, "c", 0), (2, "b", 4), (2, "b", 5), (1, "c", 1), (2, "c", 2), (2, "c", 1),
    (2, "c", 0), (1, "c", 2), (2, "c", 5), (1, "c", 3), (2, "c", 4), (2, "c", 3),
    (1, "d", 1), (2, "d", 1), (2, "d", 2), (2, "d", 0), (1, "d", 0), (2, "d", 5),
    (2, "d", 3), (2, "d", 4), (1, "d", 2), (1, "d", 3), (2, "e", 1), (1, "e", 1),
    (2, "e", 2), (1, "e", 0), (2, "e", 0), (2, "e", 5), (1, "e", 2), (2, "e", 3),
    (1, "e", 3), (2, "e", 4), (2, "f", 2), (2, "f", 1), (1, "f", 0), (1, "f", 1),
    (2, "f", 0), (1, "f", 2), (1, "g", 0), (2, "f", 5), (1, "g", 1), (2, "f", 3),
    (1, "f", 3), (2, "f", 4), (1, "g", 2), (1, "g", 3), (2, "g", 2), (2, "g", 1),
    (2, "g", 0), (2, "g", 5), (2, "g", 4), (2, "g", 3),
)
N_COPIES = 14 * (len(PIECES_TWO) + len(PIECES_ONE))


def code(x, power):
    t = x * (2.0**power)
    t2 = t * t
    return ((t2 * t2) * t2 * (t * jnp.abs(t))).astype(jnp.bfloat16)


def decode(y, power):
    y = y.astype(jnp.float32)
    quarter = lax.rsqrt(lax.rsqrt(jnp.maximum(jnp.abs(y), 2.0**-126)))
    sign = jnp.where(y < 0, -(2.0**-power), 2.0**-power)
    return quarter * lax.rsqrt(quarter) * sign


def kernel(
    d1, d2, p1, m1, p2, m2,
    np1, nm1, cv1, np2, nm2, cv2,
    d1v, d2v, pm,
    s2a, s2b, s2c, r2a, r2b, r2c,
    s1b, s1c, r1a, r1b, r1c,
    send_sem, recv_sem, load_sem,
):
    row, col, fsdp = lax.axis_index("row"), lax.axis_index("col"), lax.axis_index("fsdp")
    xh, z = row // 4, row % 4
    y, core = col // 2, col % 2

    def flip4(v, mask):
        if mask == 0:
            return v
        if mask == 1:
            return v + 1 - 2 * (v % 2)
        if mask == 3:
            return 3 - v
        return 2 - v + 2 * (v % 2)

    def row_of(mask):
        high = 1 - xh if mask & 4 else xh
        return high * 4 + flip4(z, mask & 3)

    def col_of(mask):
        low = 1 - core if mask & 1 else core
        return flip4(y, mask >> 1) * 2 + low

    def device_two(mask):
        return (row_of(mask), col, fsdp)

    def device_one(mask):
        return (row, col_of(mask), fsdp)

    orders_two = ((1, 3, 4), (3, 4, 1), (4, 1, 3))
    orders_one = ((1, 2, 6), (1, 6, 2))

    def cols(index):
        return pl.ds(pl.multiple_of(index * WIDTH, WIDTH), WIDTH)

    barrier = pltpu.get_barrier_semaphore()
    for mask in (1, 3, 4):
        pl.semaphore_signal(barrier, inc=1, device_id=device_two(mask), device_id_type=MESH)
    for mask in (1, 2, 6):
        pl.semaphore_signal(barrier, inc=1, device_id=device_one(mask), device_id_type=MESH)

    n_sent = [0]
    sent = []

    def send(src, dst, device):
        i = n_sent[0]
        n_sent[0] += 1
        if i == 0:
            pl.semaphore_wait(barrier, 6)
        copy = pltpu.make_async_remote_copy(
            src_ref=src, dst_ref=dst, send_sem=send_sem.at[i], recv_sem=recv_sem.at[i],
            device_id=device, device_id_type=MESH,
        )
        copy.start()
        sent.append(copy)
        return copy

    loads = []

    def load(src, dst):
        copy = pltpu.make_async_copy(src, dst, load_sem.at[len(loads)])
        copy.start()
        loads.append(copy)
        return copy

    loaded_two, loaded_one = {}, {}
    for k in range(max(len(PIECES_TWO), len(PIECES_ONE))):
        for pieces, loaded, hbm, vmem in (
            (PIECES_TWO, loaded_two, d2, d2v),
            (PIECES_ONE, loaded_one, d1, d1v),
        ):
            if k < len(pieces):
                rs = pl.ds(pieces[k][1], pieces[k][2])
                loaded[k] = load(hbm.at[rs], vmem.at[rs])
    loaded_pm = [load(ref, pm.at[i]) for i, ref in enumerate((p1, m1, p2, m2))]

    def over(r0, n, body):
        def step(i, carry):
            body(pl.ds(pl.multiple_of(r0 + i * STEP, STEP), STEP))
            return carry

        lax.fori_loop(0, n // STEP, step, 0)

    def block_mask(order, e):
        mask = 0
        for bit, m in zip((4, 2, 1), order):
            if e & bit:
                mask ^= m
        return mask

    class Level:
        def __init__(self, pieces, orders, index_of, device, dv, cv, loaded, param, out, sa, sb, sc, ra, rb, rc):
            self.pieces, self.orders, self.index_of, self.device = pieces, orders, index_of, device
            self.dv, self.cv, self.loaded = dv, cv, loaded
            self.param, self.out = param, out
            self.sa, self.sb, self.sc, self.ra, self.rb, self.rc = sa, sb, sc, ra, rb, rc
            self.got = {}

        def at(self, k):
            o, r0, n = self.pieces[k]
            return self.orders[o], r0, n, pl.ds(r0, n)

        def cols(self, order, e):
            return cols(self.index_of(block_mask(order, e)))

        def give(self, k, e, stage):
            order, r0, n, rs = self.at(k)
            part = self.cv.at[rs, self.cols(order, e)]
            bit = (4, 2, 1)[stage]
            self.got[k, "g", e ^ bit] = send(part, part, self.device(order[stage]))

        def ready(self, k):
            if k in self.loaded:
                self.loaded.pop(k).wait()

        def want(self, *keys):
            for key in keys:
                self.got.pop(key).wait_recv()

        def step_b(self, k):
            order, r0, n, rs = self.at(k)
            self.ready(k)
            self.want((k, "a", 3), (k, "a", 2))
            places = [(q, self.cols(order, 2 + q)) for q in (1, 0)]

            def body(s):
                for q, c in places:
                    self.sb[q, s] = code(self.dv[s, c] + self.first(self.ra[2 + q, s]), 12)

            over(r0, n, body)
            for q in (1, 0):
                self.got[k, "b", q] = send(self.sb.at[q, rs], self.rb.at[q, rs], self.device(order[1]))

        def step_c(self, k):
            order, r0, n, rs = self.at(k)
            self.want((k, "a", 1), (k, "b", 1))
            c = self.cols(order, 1)

            def body(s):
                total = self.dv[s, c] + self.first(self.ra[1, s]) + decode(self.rb[1, s], 12)
                self.sc[s] = code(total, 11)

            over(r0, n, body)
            self.got[k, "c", 0] = send(self.sc.at[rs], self.rc.at[rs], self.device(order[2]))

        def step_d(self, k):
            order, r0, n, rs = self.at(k)
            self.want((k, "a", 0), (k, "b", 0), (k, "c", 0))
            mine = self.cols(order, 0)
            i = self.param

            def body(s):
                total = self.dv[s, mine] + self.first(self.ra[0, s])
                grad = (total + decode(self.rb[0, s], 12) + decode(self.rc[s], 11)) * 0.125
                moment = 0.9 * pm[i + 1, s] + grad
                params = pm[i, s] - 0.7 * (grad + 0.9 * moment)
                self.out[1][s] = moment
                self.out[0][s] = params
                self.cv[s, mine] = params.astype(jnp.bfloat16)

            over(r0, n, body)
            self.give(k, 0, 2)
            self.give(k, 0, 1)
            self.give(k, 0, 0)

        def step_e(self, k):
            self.want((k, "g", 1))
            self.give(k, 1, 1)
            self.give(k, 1, 0)

        def step_f(self, k):
            self.want((k, "g", 2))
            self.give(k, 2, 0)
            self.want((k, "g", 3))
            self.give(k, 3, 0)

        def step_g(self, k):
            self.want(*((k, "g", e) for e in (4, 5, 6, 7)))

    class Two(Level):
        def first(self, x):
            return decode(x, 13)

        def step_a(self, k):
            order, r0, n, rs = self.at(k)
            self.ready(k)
            for pair in ((3, 2), (1, 0)):
                places = [(q, self.cols(order, 4 + q)) for q in pair]

                def body(s):
                    for q, c in places:
                        self.sa[q, s] = code(self.dv[s, c], 13)

                over(r0, n, body)
                for q in pair:
                    self.got[k, "a", q] = send(self.sa.at[q, rs], self.ra.at[q, rs], self.device(order[0]))

    class One(Level):
        def first(self, x):
            return x

        def step_a(self, k):
            order, r0, n, rs = self.at(k)
            for q in (3, 2, 1, 0):
                part = d1.at[rs, self.cols(order, 4 + q)]
                self.got[k, "a", q] = send(part, self.ra.at[q, rs], self.device(order[0]))

    two = Two(PIECES_TWO, orders_two, row_of, device_two, d2v, cv2, loaded_two, 2, (np2, nm2), s2a, s2b, s2c, r2a, r2b, r2c)
    one = One(PIECES_ONE, orders_one, col_of, device_one, d1v, cv1, loaded_one, 0, (np1, nm1), None, s1b, s1c, r1a, r1b, r1c)
    for level, step, k in PLAN:
        if step == "d" and loaded_pm:
            for copy in loaded_pm:
                copy.wait()
            loaded_pm.clear()
        getattr(two if level == 2 else one, "step_" + step)(k)
    for copy in sent:
        copy.wait_send()
    assert n_sent[0] == N_COPIES


def write_out(*refs):
    sems = refs[12]
    copies = [pltpu.make_async_copy(refs[i], refs[6 + i], sems.at[i]) for i in range(6)]
    for copy in copies:
        copy.start()
    for copy in copies:
        copy.wait()


def body(delta_one, delta_two, params_one, moment_one, params_two, moment_two):
    args = (delta_one[0, 0], delta_two[0, 0], params_one[0], moment_one[0], params_two[0], moment_two[0])
    hbm = pl.BlockSpec(memory_space=pltpu.HBM)
    vmem = pl.BlockSpec(memory_space=pltpu.VMEM)
    small = jax.ShapeDtypeStruct((ROWS, WIDTH), jnp.float32)
    wide = jax.ShapeDtypeStruct((ROWS, 8 * WIDTH), jnp.bfloat16)
    f32, bf16 = jnp.float32, jnp.bfloat16
    n_local = len(PIECES_TWO) + len(PIECES_ONE)
    outs = pl.pallas_call(
        kernel,
        out_shape=tuple(pltpu.VMEM(x.shape, x.dtype) for x in (small, small, wide, small, small, wide)),
        in_specs=[hbm] * 6,
        out_specs=[vmem] * 6,
        scratch_shapes=[
            pltpu.VMEM((ROWS, 8 * WIDTH), f32),
            pltpu.VMEM((ROWS, 8 * WIDTH), f32),
            pltpu.VMEM((4, ROWS, WIDTH), f32),
            pltpu.VMEM((4, ROWS, WIDTH), bf16),
            pltpu.VMEM((2, ROWS, WIDTH), bf16),
            pltpu.VMEM((ROWS, WIDTH), bf16),
            pltpu.VMEM((4, ROWS, WIDTH), bf16),
            pltpu.VMEM((2, ROWS, WIDTH), bf16),
            pltpu.VMEM((ROWS, WIDTH), bf16),
            pltpu.VMEM((2, ROWS, WIDTH), bf16),
            pltpu.VMEM((ROWS, WIDTH), bf16),
            pltpu.VMEM((4, ROWS, WIDTH), f32),
            pltpu.VMEM((2, ROWS, WIDTH), bf16),
            pltpu.VMEM((ROWS, WIDTH), bf16),
            pltpu.SemaphoreType.DMA((N_COPIES,)),
            pltpu.SemaphoreType.DMA((N_COPIES,)),
            pltpu.SemaphoreType.DMA((n_local + 4,)),
        ],
        compiler_params=pltpu.CompilerParams(
            collective_id=0, has_side_effects=True, vmem_limit_bytes=32 * 1024 * 1024
        ),
        name="outer_step",
    )(*(pltpu.with_memory_space_constraint(x, pltpu.HBM) for x in args))
    outs = pl.pallas_call(
        write_out,
        out_shape=(small, small, wide, small, small, wide),
        in_specs=[vmem] * 6,
        out_specs=[hbm] * 6,
        scratch_shapes=[pltpu.SemaphoreType.DMA((6,))],
        compiler_params=pltpu.CompilerParams(vmem_limit_bytes=1024 * 1024),
        name="write_out",
    )(*(pltpu.with_memory_space_constraint(x, pltpu.VMEM) for x in outs))
    return tuple(out[None] for out in outs)


def solution(mesh):
    placed = (
        P("row", "col", "fsdp", None),
        P("row", "col", "fsdp", None),
        P("row", "fsdp", "col"),
        P("row", "fsdp", "col"),
        P("col", "fsdp", "row"),
        P("col", "fsdp", "row"),
    )
    return jax.shard_map(
        body,
        mesh=mesh,
        in_specs=placed,
        out_specs=(
            P("row", "fsdp", "col"),
            P("row", "fsdp", "col"),
            P("row", "fsdp", None),
            P("col", "fsdp", "row"),
            P("col", "fsdp", "row"),
            P("col", "fsdp", None),
        ),
        check_vma=False,
    )
```

time: 430 us -> 44.7 us (0.10)
  waiting for transfers between devices: 398 us -> 0 us
  Pallas kernels: 0 us -> 43.6 us
  other arithmetic: 15.1 us -> 0 us
  between operations: 14.1 us -> 0.64 us
    all_gather x4 -> x0, waiting for transfers between devices: 218 us -> none  [the longest x1 74 us: body(): lax.all_gather(params_two, 'row', axis=2, tiled=True)]
    psum x2 -> x0, waiting for transfers between devices: 177 us -> none  [the longest x1 103 us: body(): grad_two = lax.psum(delta_two, 'row')[0] / row_count]
    pallas_call x0 -> x2, Pallas kernels: none -> 43.6 us  [the longest x1 40.8 us: body(): pl.pallas_call(kernel, out_shape=tuple((pltpu.VMEM(x.shape, x.dtype) for...]
    convert_element_type x2 -> x0, other arithmetic: 15.1 us -> none  [the longest x1 7.56 us: body(): first_copy = whole_params_one.astype(jnp.bfloat16)]
  transfers between devices with their start and end apart: 6 -> 0, of which waited for: 6 -> 0; matrix products, arithmetic and copies ran while one was open for 2% -> 0% of each run, Pallas kernels for 0% -> 0%
where the time goes in v2:
time: 44.7 us; the launch traced here: 44.2 us
  Pallas kernels  43.6 us (98%)
  between operations  0.64 us (1%)
    pallas_call x1, Pallas kernels, body(): pl.pallas_call(kernel, out_shape=tuple((pltpu.VMEM(x.shape, x.dtype) for...  40.8 us
    pallas_call x1, Pallas kernels, body(): pl.pallas_call(write_out, out_shape=(small, small, wide, small, small, wi...  2.75 us

profile of v2, /device:TPU:1, one launch (start us, length us, event | category | flops | bytes accessed | tf_op | source)
XLA Modules:
  0.0 44.2 jit_solution(14038808895705564067)
XLA Ops:
  0.6 40.8 %outer_step.1 = (f32[512,256]{1,0:T(8,128)S(1)}, f32[512,256]{1,0:T(8,128)S(1)}, bf16[512,2048]{1,0:T(8,128)(2,1)S(1)}, f32[512,256]{1,0:T(8,128)S(1)}, f32[512,...) custom-call(f32[512,2048]{1,0:T(8,128)} %bitcast.12, f32[512,2048]{1,0:T(8,128)} %bitcast.13, f32[512,256]{1,0:T(8,128)} %bitcast.14, ...), custom_call_target="tpu_custom_call" | custom-call | tf_op jit(solution)/shard_map/outer_step/pallas_call | solution.py:286
  41.5 2.8 %write_out.1 = (f32[512,256]{1,0:T(8,128)}, f32[512,256]{1,0:T(8,128)}, bf16[512,2048]{1,0:T(8,128)(2,1)}, f32[512,256]{1,0:T(8,128)}, f32[512,256]{1,0:T(8,128)}, /*index=5*/bf16[512,2048]{1,0:T(8,128)(2,1)}) custom-call(f32[512,256]{1,0:T(8,128)S(1)} %get-tuple-element.18.refs_0_, f32[512,256]{1,0:T(8,128)S(1)} %get-tuple-element.19.refs_1_, ...), custom_call_target="tpu_custom_call" | custom-call | tf_op jit(solution)/shard_map/write_out/pallas_call | solution.py:315

commit v3 on v2

--- a/solution.py
+++ b/solution.py
@@ -8,23 +8,34 @@
 MESH = pl.DeviceIdType.MESH
 ROWS, WIDTH = 512, 256
 STEP = 16
-PIECES_TWO = ((0, 0, 96), (1, 96, 96), (2, 192, 80), (0, 272, 80), (1, 352, 80), (2, 432, 80))
-PIECES_ONE = ((0, 0, 128), (1, 128, 128), (0, 256, 128), (1, 384, 128))
+PIECES_TWO = ((0, 0, 64), (1, 64, 64), (2, 128, 48), (0, 176, 80), (1, 256, 64), (2, 320, 64), (0, 384, 48), (1, 432, 48), (2, 480, 32))
+PIECES_ONE = ((0, 0, 96), (1, 96, 96), (0, 192, 160), (1, 352, 160))
 PLAN = (
-    (2, "a", 0), (2, "a", 1), (2, "a", 2), (2, "a", 3), (2, "a", 4), (2, "a", 5),
-    (1, "a", 0), (1, "a", 1), (1, "a", 2), (1, "a", 3), (2, "b", 0), (2, "b", 1),
-    (2, "b", 2), (1, "b", 0), (1, "b", 1), (1, "b", 2), (2, "b", 3), (1, "b", 3),
-    (1, "c", 0), (2, "b", 4), (2, "b", 5), (1, "c", 1), (2, "c", 2), (2, "c", 1),
-    (2, "c", 0), (1, "c", 2), (2, "c", 5), (1, "c", 3), (2, "c", 4), (2, "c", 3),
-    (1, "d", 1), (2, "d", 1), (2, "d", 2), (2, "d", 0), (1, "d", 0), (2, "d", 5),
-    (2, "d", 3), (2, "d", 4), (1, "d", 2), (1, "d", 3), (2, "e", 1), (1, "e", 1),
-    (2, "e", 2), (1, "e", 0), (2, "e", 0), (2, "e", 5), (1, "e", 2), (2, "e", 3),
-    (1, "e", 3), (2, "e", 4), (2, "f", 2), (2, "f", 1), (1, "f", 0), (1, "f", 1),
-    (2, "f", 0), (1, "f", 2), (1, "g", 0), (2, "f", 5), (1, "g", 1), (2, "f", 3),
-    (1, "f", 3), (2, "f", 4), (1, "g", 2), (1, "g", 3), (2, "g", 2), (2, "g", 1),
-    (2, "g", 0), (2, "g", 5), (2, "g", 4), (2, "g", 3),
+    (2, "a3", 0), (1, "a3", 0), (2, "a3", 1), (2, "a21", 0), (2, "a21", 1), (2, "a3", 2),
+    (2, "a21", 2), (1, "a3", 2), (2, "a0", 0), (2, "a3", 3), (2, "a0", 1), (1, "b1", 0),
+    (1, "b1", 1), (2, "a3", 4), (2, "a3", 5), (1, "b0", 0), (2, "a0", 2), (1, "b0", 1),
+    (2, "a3", 6), (2, "a3", 7), (2, "a3", 8), (2, "a21", 3), (2, "b1", 0), (2, "a21", 4),
+    (2, "a21", 5), (2, "b1", 1), (2, "b1", 2), (1, "b1", 2), (1, "b1", 3), (2, "b0", 0),
+    (1, "b0", 2), (2, "b0", 1), (2, "b0", 2), (1, "b0", 3), (1, "c", 0), (1, "c", 1),
+    (2, "b1", 5), (2, "b1", 3), (2, "b1", 4), (2, "b1", 6), (2, "b1", 8), (2, "b1", 7),
+    (2, "a0", 3), (2, "a0", 4), (2, "a0", 5), (2, "a21", 6), (2, "c", 0), (2, "b0", 5),
+    (2, "a21", 7), (2, "b0", 3), (2, "a21", 8), (2, "c", 1), (2, "c", 2), (1, "c", 2),
+    (1, "c", 3), (2, "b0", 4), (2, "a0", 6), (2, "a0", 7), (2, "a0", 8), (2, "c", 4),
+    (2, "c", 5), (2, "c", 3), (1, "d", 1), (1, "d", 0), (2, "d", 0), (2, "c", 6),
+    (2, "c", 7), (2, "c", 8), (2, "b0", 6), (2, "b0", 7), (2, "b0", 8), (2, "d", 1),
+    (2, "d", 2), (2, "d", 3), (2, "d", 4), (2, "d", 5), (1, "d", 2), (1, "d", 3),
+    (2, "d", 6), (2, "d", 7), (2, "d", 8), (1, "e", 0), (1, "e", 1), (2, "e", 0),
+    (2, "e", 1), (2, "e", 2), (2, "e", 3), (2, "e", 4), (2, "e", 5), (1, "e", 2),
+    (2, "e", 6), (2, "e", 7), (2, "e", 8), (1, "e", 3), (2, "f", 0), (2, "f", 1),
+    (2, "f", 2), (1, "f", 0), (1, "f", 1), (2, "f", 4), (2, "f", 3), (2, "f", 5),
+    (2, "f", 7), (1, "g", 0), (1, "g", 1), (1, "f", 2), (2, "f", 6), (2, "f", 8),
+    (1, "f", 3), (2, "g", 0), (2, "g", 1), (2, "g", 2), (1, "g", 2), (1, "g", 3),
+    (2, "g", 3), (2, "g", 4), (2, "g", 5), (2, "g", 7), (2, "g", 6), (2, "g", 8),
 )
-N_COPIES = 14 * (len(PIECES_TWO) + len(PIECES_ONE))
+LOADS = ((2, 0), (2, 1), (2, 2), (2, 3), (1, 0), (1, 1), (2, 4), (2, 5), (2, 6), (2, 7), (2, 8), (1, 2), (1, 3))
+FIRST_LOADS = 2
+DRAIN = {"d": ("a3", "a21", "a0", "b1"), "e": ("b0", "c"), "f": ("d",), "g": ("e",)}
+N_COPIES = 13 * len(PIECES_TWO) + 12 * len(PIECES_ONE)
 
 
 def code(x, power):
@@ -52,6 +63,8 @@
     xh, z = row // 4, row % 4
     y, core = col // 2, col % 2
 
+    known = {}
+
     def flip4(v, mask):
         if mask == 0:
             return v
@@ -62,12 +75,20 @@
         return 2 - v + 2 * (v % 2)
 
     def row_of(mask):
-        high = 1 - xh if mask & 4 else xh
-        return high * 4 + flip4(z, mask & 3)
+        if ("row", mask) not in known:
+            high = 1 - xh if mask & 4 else xh
+            known["row", mask] = high * 4 + flip4(z, mask & 3)
+        return known["row", mask]
 
     def col_of(mask):
-        low = 1 - core if mask & 1 else core
-        return flip4(y, mask >> 1) * 2 + low
+        if ("col", mask) not in known:
+            low = 1 - core if mask & 1 else core
+            known["col", mask] = flip4(y, mask >> 1) * 2 + low
+        return known["col", mask]
+
+    for mask in range(8):
+        row_of(mask)
+        col_of(mask)
 
     def device_two(mask):
         return (row_of(mask), col, fsdp)
@@ -103,24 +124,31 @@
         sent.append(copy)
         return copy
 
+    def drain(copies):
+        for copy in copies:
+            copy.wait_send()
+
     loads = []
 
     def load(src, dst):
         copy = pltpu.make_async_copy(src, dst, load_sem.at[len(loads)])
-        copy.start()
         loads.append(copy)
         return copy
 
+    n_started = [0]
+
+    def start_loads(count):
+        for copy in loads[n_started[0] : n_started[0] + count]:
+            copy.start()
+        n_started[0] = min(n_started[0] + count, len(loads))
+
     loaded_two, loaded_one = {}, {}
-    for k in range(max(len(PIECES_TWO), len(PIECES_ONE))):
-        for pieces, loaded, hbm, vmem in (
-            (PIECES_TWO, loaded_two, d2, d2v),
-            (PIECES_ONE, loaded_one, d1, d1v),
-        ):
-            if k < len(pieces):
-                rs = pl.ds(pieces[k][1], pieces[k][2])
-                loaded[k] = load(hbm.at[rs], vmem.at[rs])
+    for level, k in LOADS:
+        pieces, loaded, hbm, vmem = (PIECES_TWO, loaded_two, d2, d2v) if level == 2 else (PIECES_ONE, loaded_one, d1, d1v)
+        rs = pl.ds(pieces[k][1], pieces[k][2])
+        loaded[k] = load(hbm.at[rs], vmem.at[rs])
     loaded_pm = [load(ref, pm.at[i]) for i, ref in enumerate((p1, m1, p2, m2))]
+    start_loads(FIRST_LOADS)
 
     def over(r0, n, body):
         def step(i, carry):
@@ -159,33 +187,42 @@
 
         def ready(self, k):
             if k in self.loaded:
-                self.loaded.pop(k).wait()
+                copy = self.loaded.pop(k)
+                while not any(copy is started for started in loads[: n_started[0]]):
+                    start_loads(1)
+                copy.wait()
 
         def want(self, *keys):
             for key in keys:
-                self.got.pop(key).wait_recv()
-
-        def step_b(self, k):
+                if key in self.got:
+                    self.got.pop(key).wait_recv()
+
+        def second(self, k, q):
             order, r0, n, rs = self.at(k)
             self.ready(k)
-            self.want((k, "a", 3), (k, "a", 2))
-            places = [(q, self.cols(order, 2 + q)) for q in (1, 0)]
+            self.want(self.first_key(k, 2 + q))
+            c = self.cols(order, 2 + q)
+            came = self.slot(k, 2 + q)
 
             def body(s):
-                for q, c in places:
-                    self.sb[q, s] = code(self.dv[s, c] + self.first(self.ra[2 + q, s]), 12)
+                self.sb[q, s] = code(self.dv[s, c] + self.first(self.ra[came, s]), 12)
 
             over(r0, n, body)
-            for q in (1, 0):
-                self.got[k, "b", q] = send(self.sb.at[q, rs], self.rb.at[q, rs], self.device(order[1]))
+            self.got[k, "b", q] = send(self.sb.at[q, rs], self.rb.at[q, rs], self.device(order[1]))
+
+        def step_b1(self, k):
+            self.second(k, 1)
+
+        def step_b0(self, k):
+            self.second(k, 0)
 
         def step_c(self, k):
             order, r0, n, rs = self.at(k)
-            self.want((k, "a", 1), (k, "b", 1))
+            self.want(self.first_key(k, 1), (k, "b", 1))
             c = self.cols(order, 1)
 
             def body(s):
-                total = self.dv[s, c] + self.first(self.ra[1, s]) + decode(self.rb[1, s], 12)
+                total = self.dv[s, c] + self.first(self.ra[self.slot(k, 1), s]) + decode(self.rb[1, s], 12)
                 self.sc[s] = code(total, 11)
 
             over(r0, n, body)
@@ -193,7 +230,7 @@
 
         def step_d(self, k):
             order, r0, n, rs = self.at(k)
-            self.want((k, "a", 0), (k, "b", 0), (k, "c", 0))
+            self.want(self.first_key(k, 0), (k, "b", 0), (k, "c", 0))
             mine = self.cols(order, 0)
             i = self.param
 
@@ -229,40 +266,69 @@
         def first(self, x):
             return decode(x, 13)
 
-        def step_a(self, k):
+        def slot(self, k, q):
+            return q
+
+        def first_key(self, k, q):
+            return (k, "a", (0, 1, 1, 3)[q])
+
+        def first_send(self, k, low, count):
             order, r0, n, rs = self.at(k)
             self.ready(k)
-            for pair in ((3, 2), (1, 0)):
-                places = [(q, self.cols(order, 4 + q)) for q in pair]
-
-                def body(s):
-                    for q, c in places:
-                        self.sa[q, s] = code(self.dv[s, c], 13)
-
-                over(r0, n, body)
-                for q in pair:
-                    self.got[k, "a", q] = send(self.sa.at[q, rs], self.ra.at[q, rs], self.device(order[0]))
+            places = [(q, self.cols(order, 4 + q)) for q in range(low, low + count)]
+
+            def body(s):
+                for q, c in places:
+                    self.sa[q, s] = code(self.dv[s, c], 13)
+
+            over(r0, n, body)
+            slots = pl.ds(low, count)
+            self.got[k, "a", low] = send(self.sa.at[slots, rs], self.ra.at[slots, rs], self.device(order[0]))
+
+        def step_a3(self, k):
+            self.first_send(k, 3, 1)
+
+        def step_a21(self, k):
+            self.first_send(k, 1, 2)
+
+        def step_a0(self, k):
+            self.first_send(k, 0, 1)
 
     class One(Level):
         def first(self, x):
             return x
 
-        def step_a(self, k):
-            order, r0, n, rs = self.at(k)
+        def slot(self, k, q):
+            return q if k % 2 == 0 else (0, 2, 1, 3)[q]
+
+        def first_key(self, k, q):
+            return (k // 2, "a", self.slot(k, q))
+
+        def step_a3(self, k):
+            order, r0, n, rs = self.at(k)
+            if k % 2:
+                return
+            rs = pl.ds(r0, n + self.pieces[k + 1][2])
             for q in (3, 2, 1, 0):
                 part = d1.at[rs, self.cols(order, 4 + q)]
-                self.got[k, "a", q] = send(part, self.ra.at[q, rs], self.device(order[0]))
+                self.got[k // 2, "a", q] = send(part, self.ra.at[q, rs], self.device(order[0]))
 
     two = Two(PIECES_TWO, orders_two, row_of, device_two, d2v, cv2, loaded_two, 2, (np2, nm2), s2a, s2b, s2c, r2a, r2b, r2c)
     one = One(PIECES_ONE, orders_one, col_of, device_one, d1v, cv1, loaded_one, 0, (np1, nm1), None, s1b, s1c, r1a, r1b, r1c)
+    unsent = {}
     for level, step, k in PLAN:
         if step == "d" and loaded_pm:
             for copy in loaded_pm:
                 copy.wait()
             loaded_pm.clear()
         getattr(two if level == 2 else one, "step_" + step)(k)
-    for copy in sent:
-        copy.wait_send()
+        start_loads(2)
+        unsent[level, k, step] = tuple(sent)
+        sent.clear()
+        for early in DRAIN.get(step, ()):
+            drain(unsent.pop((level, k, early), ()))
+    for copies in unsent.values():
+        drain(copies)
     assert n_sent[0] == N_COPIES
 
 

time: 44.7 us -> 43.4 us (0.971)
  Pallas kernels: 43.6 us -> 42 us
    pallas_call x1, Pallas kernels: 40.8 us -> 39.2 us  [body(): pl.pallas_call(kernel, out_shape=tuple((pltpu.VMEM(x.shape, x.dtype) for...]
where the time goes in v3:
time: 43.4 us; the launch traced here: 42.6 us
  Pallas kernels  42 us (97%)
  between operations  0.64 us (1%)
    pallas_call x1, Pallas kernels, body(): pl.pallas_call(kernel, out_shape=tuple((pltpu.VMEM(x.shape, x.dtype) for...  39.2 us
    pallas_call x1, Pallas kernels, body(): pl.pallas_call(write_out, out_shape=(small, small, wide, small, small, wi...  2.75 us

profile of v3, /device:TPU:1, one launch (start us, length us, event | category | flops | bytes accessed | tf_op | source)
XLA Modules:
  0.0 42.6 jit_solution(812490980810781381)
XLA Ops:
  0.6 39.2 %outer_step.1 = (f32[512,256]{1,0:T(8,128)S(1)}, f32[512,256]{1,0:T(8,128)S(1)}, bf16[512,2048]{1,0:T(8,128)(2,1)S(1)}, f32[512,256]{1,0:T(8,128)S(1)}, f32[512,...) custom-call(f32[512,2048]{1,0:T(8,128)} %bitcast.12, f32[512,2048]{1,0:T(8,128)} %bitcast.13, f32[512,256]{1,0:T(8,128)} %bitcast.14, ...), custom_call_target="tpu_custom_call" | custom-call | tf_op jit(solution)/shard_map/outer_step/pallas_call | solution.py:352
  39.9 2.8 %write_out.1 = (f32[512,256]{1,0:T(8,128)}, f32[512,256]{1,0:T(8,128)}, bf16[512,2048]{1,0:T(8,128)(2,1)}, f32[512,256]{1,0:T(8,128)}, f32[512,256]{1,0:T(8,128)}, /*index=5*/bf16[512,2048]{1,0:T(8,128)(2,1)}) custom-call(f32[512,256]{1,0:T(8,128)S(1)} %get-tuple-element.18.refs_0_, f32[512,256]{1,0:T(8,128)S(1)} %get-tuple-element.19.refs_1_, ...), custom_call_target="tpu_custom_call" | custom-call | tf_op jit(solution)/shard_map/write_out/pallas_call | solution.py:381

commit v4 on v3

v4 whole, which is shorter than its diff:
```python
import jax
import jax.numpy as jnp
from jax import lax
from jax.experimental import pallas as pl
from jax.experimental.pallas import tpu as pltpu
from jax.sharding import PartitionSpec as P

MESH = pl.DeviceIdType.MESH
ROWS, WIDTH = 512, 256
STEP = 16
PIECES_TWO = ((0, 0, 80), (1, 80, 80), (2, 160, 64), (0, 224, 96), (1, 320, 96), (2, 416, 96))
PIECES_ONE = ((0, 0, 176), (0, 176, 176), (0, 352, 160))
PLAN = (
    (2, "a3", 0), (2, "a21", 0), (1, "a3", 0), (2, "a3", 1), (2, "a21", 1), (1, "a3", 1),
    (2, "a3", 2), (2, "a21", 2), (1, "a3", 2), (2, "a3", 3), (2, "a3", 4), (2, "a3", 5),
    (2, "b1", 0), (2, "a21", 3), (1, "b1", 0), (2, "b1", 1), (2, "b1", 2), (2, "a21", 4),
    (2, "a21", 5), (2, "b0", 0), (2, "b0", 1), (1, "b1", 1), (2, "b1", 3), (2, "b1", 4),
    (2, "b1", 5), (2, "b0", 2), (2, "c", 0), (2, "c", 1), (1, "b1", 2), (2, "c", 2),
    (2, "b0", 3), (2, "a0", 0), (2, "b0", 4), (2, "b0", 5), (2, "a0", 1), (2, "c", 5),
    (2, "a0", 2), (2, "a0", 3), (1, "d", 0), (2, "c", 3), (2, "c", 4), (2, "a0", 4),
    (2, "d", 0), (2, "a0", 5), (2, "d", 1), (1, "d", 1), (2, "d", 2), (2, "d", 3),
    (2, "d", 4), (2, "d", 5), (1, "d", 2), (2, "e", 0), (2, "e", 1), (2, "e", 2),
    (2, "e", 3), (2, "e", 4), (1, "e", 0), (2, "e", 5), (2, "f", 0), (2, "f", 1),
    (2, "f", 2), (2, "f", 3), (2, "f", 4), (1, "g", 0), (2, "f", 5), (1, "e", 1),
    (2, "g", 0), (2, "g", 1), (2, "g", 2), (1, "e", 2), (1, "g", 1), (2, "g", 3),
    (2, "g", 4), (2, "g", 5), (1, "g", 2),
)
ORDERS = ((1, 3, 4), (3, 4, 1), (4, 1, 3))
LOADS = ((2, 0), (2, 1), (2, 2), (2, 3), (2, 4), (2, 5), (1, 0), (1, 1), (1, 2))
FIRST_LOADS = 2
KINDS = 4
ARRIVALS = 7 * len(PIECES_TWO) + 4 * len(PIECES_ONE)


def code(x, power):
    t = x * (2.0**power)
    t2 = t * t
    return ((t2 * t2) * t2 * (t * jnp.abs(t))).astype(jnp.bfloat16)


def decode(y, power):
    y = y.astype(jnp.float32)
    quarter = lax.rsqrt(lax.rsqrt(jnp.maximum(jnp.abs(y), 2.0**-126)))
    sign = jnp.where(y < 0, -(2.0**-power), 2.0**-power)
    return quarter * lax.rsqrt(quarter) * sign


def kernel(
    d1, d2, p1, m1, p2, m2,
    np1, nm1, cv1, np2, nm2, cv2,
    d1v, d2v, pm,
    s2a, s2b, s2c, r2a, r2b, r2c,
    s1b, r1a, r1b,
    send_sem, recv_sem, load_sem,
):
    row, col, fsdp = lax.axis_index("row"), lax.axis_index("col"), lax.axis_index("fsdp")
    xh, z = row // 4, row % 4
    y, core = col // 2, col % 2

    known = {}

    def flip4(v, mask):
        if mask == 0:
            return v
        if mask == 1:
            return v + 1 - 2 * (v % 2)
        if mask == 3:
            return 3 - v
        return 2 - v + 2 * (v % 2)

    def row_of(mask):
        if ("row", mask) not in known:
            high = 1 - xh if mask & 4 else xh
            known["row", mask] = high * 4 + flip4(z, mask & 3)
        return known["row", mask]

    def col_of(mask):
        if ("col", mask) not in known:
            low = 1 - core if mask & 1 else core
            known["col", mask] = flip4(y, mask >> 1) * 2 + low
        return known["col", mask]

    for mask in range(8):
        row_of(mask)
        col_of(mask)

    def device_two(mask):
        return (row_of(mask), col, fsdp)

    def device_one(mask):
        return (row, col_of(mask), fsdp)

    def cols(index):
        return pl.ds(pl.multiple_of(index * WIDTH, WIDTH), WIDTH)

    barrier = pltpu.get_barrier_semaphore()
    for mask in (1, 3, 4):
        pl.semaphore_signal(barrier, inc=1, device_id=device_two(mask), device_id_type=MESH)
    for mask in (1, 2, 4, 6):
        pl.semaphore_signal(barrier, inc=1, device_id=device_one(mask), device_id_type=MESH)

    def block_mask(order, e):
        mask = 0
        for bit, m in zip((4, 2, 1), order):
            if e & bit:
                mask ^= m
        return mask

    arrivals = {}

    def arrival(key):
        return recv_sem.at[arrivals.setdefault(key, len(arrivals))]

    def send(src, dst, device, kind, key):
        if not arrivals:
            pl.semaphore_wait(barrier, 7)
        pltpu.make_async_remote_copy(
            src_ref=src, dst_ref=dst, send_sem=send_sem.at[kind], recv_sem=arrival(key),
            device_id=device, device_id_type=MESH,
        ).start()

    def wait_bytes(sem, ref):
        pltpu.make_async_copy(ref, ref, sem).wait()

    loads = []

    def load(src, dst):
        copy = pltpu.make_async_copy(src, dst, load_sem.at[len(loads)])
        loads.append(copy)
        return copy

    n_started = [0]

    def start_loads(count):
        for copy in loads[n_started[0] : n_started[0] + count]:
            copy.start()
        n_started[0] = min(n_started[0] + count, len(loads))

    loaded_two, loaded_one = {}, {}
    for level, k in LOADS:
        pieces, loaded, hbm, vmem = (PIECES_TWO, loaded_two, d2, d2v) if level == 2 else (PIECES_ONE, loaded_one, d1, d1v)
        rs = pl.ds(pieces[k][1], pieces[k][2])
        loaded[k] = load(hbm.at[rs], vmem.at[rs])
    n_rows = len(loads)
    for i, ref in enumerate((p1, m1, p2, m2)):
        loads.append(pltpu.make_async_copy(ref, pm.at[i], load_sem.at[n_rows]))
    start_loads(FIRST_LOADS)

    def over(r0, n, body):
        def step(i, carry):
            body(pl.ds(pl.multiple_of(r0 + i * STEP, STEP), STEP))
            return carry

        lax.fori_loop(0, n // STEP, step, 0)

    class Level:
        def __init__(self, pieces, index_of, device, dv, cv, loaded, param, out, buffers):
            self.pieces, self.index_of, self.device = pieces, index_of, device
            self.dv, self.cv, self.loaded = dv, cv, loaded
            self.param, self.out = param, out
            self.sa, self.sb, self.sc, self.ra, self.rb, self.rc = buffers
            self.waited = set()

        def rows(self, k):
            r0, n = self.pieces[k][1:]
            return r0, n, pl.ds(r0, n)

        def cols(self, mask):
            return cols(self.index_of(mask))

        def ready(self, k):
            if k in self.loaded:
                copy = self.loaded.pop(k)
                while not any(copy is started for started in loads[: n_started[0]]):
                    start_loads(1)
                copy.wait()

        def want(self, k, name, ref):
            key = (self.param, k, name)
            if key not in self.waited:
                self.waited.add(key)
                wait_bytes(arrival(key), ref)

        def want_blocks(self, k, name, count):
            self.want(k, name, self.cv.at[self.rows(k)[2], pl.ds(0, count * WIDTH)])

        def put(self, k, src, dst, link, kind, name):
            send(src, dst, self.device(link), kind + KINDS * (self.param // 2), (self.param, k, name))

        def give(self, k, mask, link, name):
            part = self.cv.at[self.rows(k)[2], self.cols(mask)]
            self.put(k, part, part, link, 3, name)

        def finish(self, k, total_of):
            r0, n, rs = self.rows(k)
            mine = self.cols(0)
            i = self.param

            def body(s):
                grad = (self.dv[s, mine] + total_of(s)) * 0.125
                moment = 0.9 * pm[i + 1, s] + grad
                params = pm[i, s] - 0.7 * (grad + 0.9 * moment)
                self.out[1][s] = moment
                self.out[0][s] = params
                self.cv[s, mine] = params.astype(jnp.bfloat16)

            over(r0, n, body)

    class Two(Level):
        def masks(self, k):
            return ORDERS[self.pieces[k][0]]

        def block(self, k, e):
            return block_mask(self.masks(k), e)

        def first_send(self, k, low, count, name):
            r0, n, rs = self.rows(k)
            self.ready(k)
            places = [(q, self.cols(self.block(k, 4 + q))) for q in range(low, low + count)]

            def body(s):
                for q, c in places:
                    self.sa[q, s] = code(self.dv[s, c], 13)

            over(r0, n, body)
            slots = pl.ds(low, count)
            self.put(k, self.sa.at[slots, rs], self.ra.at[slots, rs], self.masks(k)[0], 0, name)

        def step_a3(self, k):
            self.first_send(k, 3, 1, "a3")

        def step_a21(self, k):
            self.first_send(k, 1, 2, "a21")

        def step_a0(self, k):
            self.first_send(k, 0, 1, "last")

        def want_21(self, k):
            self.want(k, "a21", self.ra.at[pl.ds(1, 2), self.rows(k)[2]])

        def second(self, k, q, name):
            r0, n, rs = self.rows(k)
            c = self.cols(self.block(k, 2 + q))

            def body(s):
                self.sb[q, s] = code(self.dv[s, c] + decode(self.ra[2 + q, s], 13), 12)

            over(r0, n, body)
            self.put(k, self.sb.at[q, rs], self.rb.at[q, rs], self.masks(k)[1], 1, name)

        def step_b1(self, k):
            self.want(k, "a3", self.ra.at[3, self.rows(k)[2]])
            self.second(k, 1, "b1")

        def step_b0(self, k):
            self.want_21(k)
            self.second(k, 0, "last")

        def step_c(self, k):
            r0, n, rs = self.rows(k)
            self.want_21(k)
            self.want(k, "b1", self.rb.at[1, rs])
            c = self.cols(self.block(k, 1))

            def body(s):
                self.sc[s] = code(self.dv[s, c] + decode(self.ra[1, s], 13) + decode(self.rb[1, s], 12), 11)

            over(r0, n, body)
            self.put(k, self.sc.at[rs], self.rc.at[rs], self.masks(k)[2], 2, "last")

        def step_d(self, k):
            self.want_blocks(k, "last", 3)
            self.finish(k, lambda s: decode(self.ra[0, s], 13) + decode(self.rb[0, s], 12) + decode(self.rc[s], 11))
            one, two, three = self.masks(k)
            self.give(k, 0, three, "e")
            self.give(k, 0, two, "e")
            self.give(k, 0, one, "g")

        def step_e(self, k):
            one, two, three = self.masks(k)
            self.want_blocks(k, "e", 2)
            self.give(k, three, two, "f")
            self.give(k, three, one, "g")
            self.give(k, two, one, "g")

        def step_f(self, k):
            one, two, three = self.masks(k)
            self.want_blocks(k, "f", 1)
            self.give(k, two ^ three, one, "g")

        def step_g(self, k):
            self.want_blocks(k, "g", 4)

    class One(Level):
        def step_a3(self, k):
            rs = self.rows(k)[2]
            for chip in (2, 1, 3, 0):
                part = d1.at[rs, self.cols(2 * chip + 1)]
                self.put(k, part, self.ra.at[chip, rs], 1, 0, "last" if chip == 0 else "a")

        def step_b1(self, k):
            r0, n, rs = self.rows(k)
            self.ready(k)
            self.want(k, "a", self.ra.at[pl.ds(1, 3), rs])
            places = [(chip, self.cols(2 * chip)) for chip in (2, 1, 3)]

            def body(s):
                for chip, c in places:
                    self.sb[chip - 1, s] = code(self.dv[s, c] + self.ra[chip, s], 12)

            over(r0, n, body)
            for chip in (2, 1, 3):
                slot = chip - 1
                self.put(k, self.sb.at[slot, rs], self.rb.at[slot, rs], 2 * chip, 1, "last")

        def step_d(self, k):
            self.want_blocks(k, "last", 5)
            self.finish(k, lambda s: self.ra[0, s] + sum(decode(self.rb[slot, s], 12) for slot in range(3)))
            for chip in (2, 1, 3):
                self.give(k, 0, 2 * chip, "e")
            self.give(k, 0, 1, "g")

        def step_e(self, k):
            self.want_blocks(k, "e", 3)
            for chip in (1, 3, 2):
                self.give(k, 2 * chip, 1, "g")

        def step_g(self, k):
            self.want_blocks(k, "g", 4)

    two = Two(PIECES_TWO, row_of, device_two, d2v, cv2, loaded_two, 2, (np2, nm2), (s2a, s2b, s2c, r2a, r2b, r2c))
    one = One(PIECES_ONE, col_of, device_one, d1v, cv1, loaded_one, 0, (np1, nm1), (None, s1b, None, r1a, r1b, None))
    loaded_pm = False
    for level, step, k in PLAN:
        if step == "d" and not loaded_pm:
            start_loads(4)
            wait_bytes(load_sem.at[n_rows], pm)
            loaded_pm = True
        getattr(two if level == 2 else one, "step_" + step)(k)
        start_loads(2)
    gathered = pl.ds(0, 7 * WIDTH)
    sources = (r1a, s1b, None, cv1.at[:, gathered], s2a, s2b, s2c, cv2.at[:, gathered])
    for kind, source in enumerate(sources):
        if source is not None:
            wait_bytes(send_sem.at[kind], source)
    assert len(arrivals) == ARRIVALS


def write_out(*refs):
    sems = refs[12]
    copies = [pltpu.make_async_copy(refs[i], refs[6 + i], sems.at[i]) for i in range(6)]
    for copy in copies:
        copy.start()
    for copy in copies:
        copy.wait()


def body(delta_one, delta_two, params_one, moment_one, params_two, moment_two):
    args = (delta_one[0, 0], delta_two[0, 0], params_one[0], moment_one[0], params_two[0], moment_two[0])
    hbm = pl.BlockSpec(memory_space=pltpu.HBM)
    vmem = pl.BlockSpec(memory_space=pltpu.VMEM)
    small = jax.ShapeDtypeStruct((ROWS, WIDTH), jnp.float32)
    wide = jax.ShapeDtypeStruct((ROWS, 8 * WIDTH), jnp.bfloat16)
    f32, bf16 = jnp.float32, jnp.bfloat16
    n_local = len(PIECES_TWO) + len(PIECES_ONE)
    outs = pl.pallas_call(
        kernel,
        out_shape=tuple(pltpu.VMEM(x.shape, x.dtype) for x in (small, small, wide, small, small, wide)),
        in_specs=[hbm] * 6,
        out_specs=[vmem] * 6,
        scratch_shapes=[
            pltpu.VMEM((ROWS, 8 * WIDTH), f32),
            pltpu.VMEM((ROWS, 8 * WIDTH), f32),
            pltpu.VMEM((4, ROWS, WIDTH), f32),
            pltpu.VMEM((4, ROWS, WIDTH), bf16),
            pltpu.VMEM((2, ROWS, WIDTH), bf16),
            pltpu.VMEM((ROWS, WIDTH), bf16),
            pltpu.VMEM((4, ROWS, WIDTH), bf16),
            pltpu.VMEM((2, ROWS, WIDTH), bf16),
            pltpu.VMEM((ROWS, WIDTH), bf16),
            pltpu.VMEM((3, ROWS, WIDTH), bf16),
            pltpu.VMEM((4, ROWS, WIDTH), f32),
            pltpu.VMEM((3, ROWS, WIDTH), bf16),
            pltpu.SemaphoreType.DMA((2 * KINDS,)),
            pltpu.SemaphoreType.DMA((ARRIVALS,)),
            pltpu.SemaphoreType.DMA((n_local + 1,)),
        ],
        compiler_params=pltpu.CompilerParams(
            collective_id=0, has_side_effects=True, vmem_limit_bytes=32 * 1024 * 1024
        ),
        name="outer_step",
    )(*(pltpu.with_memory_space_constraint(x, pltpu.HBM) for x in args))
    outs = pl.pallas_call(
        write_out,
        out_shape=(small, small, wide, small, small, wide),
        in_specs=[vmem] * 6,
        out_specs=[hbm] * 6,
        scratch_shapes=[pltpu.SemaphoreType.DMA((6,))],
        compiler_params=pltpu.CompilerParams(vmem_limit_bytes=1024 * 1024),
        name="write_out",
    )(*(pltpu.with_memory_space_constraint(x, pltpu.VMEM) for x in outs))
    return tuple(out[None] for out in outs)


def solution(mesh):
    placed = (
        P("row", "col", "fsdp", None),
        P("row", "col", "fsdp", None),
        P("row", "fsdp", "col"),
        P("row", "fsdp", "col"),
        P("col", "fsdp", "row"),
        P("col", "fsdp", "row"),
    )
    return jax.shard_map(
        body,
        mesh=mesh,
        in_specs=placed,
        out_specs=(
            P("row", "fsdp", "col"),
            P("row", "fsdp", "col"),
            P("row", "fsdp", None),
            P("col", "fsdp", "row"),
            P("col", "fsdp", "row"),
            P("col", "fsdp", None),
        ),
        check_vma=False,
    )
```

time: 43.4 us -> 42.1 us (0.970); the launches traced: 42.6 us -> 42 us
  Pallas kernels: 42 us -> 41.3 us
    pallas_call x1, Pallas kernels: 39.2 us -> 38.6 us  [body(): pl.pallas_call(kernel, out_shape=tuple((pltpu.VMEM(x.shape, x.dtype) for...]
where the time goes in v4:
time: 42.1 us; the launch traced here: 42 us
  Pallas kernels  41.3 us (98%)
  between operations  0.64 us (2%)
    pallas_call x1, Pallas kernels, body(): pl.pallas_call(kernel, out_shape=tuple((pltpu.VMEM(x.shape, x.dtype) for...  38.6 us
    pallas_call x1, Pallas kernels, body(): pl.pallas_call(write_out, out_shape=(small, small, wide, small, small, wi...  2.75 us

profile of v4, /device:TPU:1, one launch (start us, length us, event | category | flops | bytes accessed | tf_op | source)
XLA Modules:
  0.0 42.0 jit_solution(16424331942717781102)
XLA Ops:
  0.6 38.6 %outer_step.1 = (f32[512,256]{1,0:T(8,128)S(1)}, f32[512,256]{1,0:T(8,128)S(1)}, bf16[512,2048]{1,0:T(8,128)(2,1)S(1)}, f32[512,256]{1,0:T(8,128)S(1)}, f32[512,...) custom-call(f32[512,2048]{1,0:T(8,128)} %bitcast.12, f32[512,2048]{1,0:T(8,128)} %bitcast.13, f32[512,256]{1,0:T(8,128)} %bitcast.14, ...), custom_call_target="tpu_custom_call" | custom-call | tf_op jit(solution)/shard_map/outer_step/pallas_call | solution.py:366
  39.2 2.8 %write_out.1 = (f32[512,256]{1,0:T(8,128)}, f32[512,256]{1,0:T(8,128)}, bf16[512,2048]{1,0:T(8,128)(2,1)}, f32[512,256]{1,0:T(8,128)}, f32[512,256]{1,0:T(8,128)}, /*index=5*/bf16[512,2048]{1,0:T(8,128)(2,1)}) custom-call(f32[512,256]{1,0:T(8,128)S(1)} %get-tuple-element.18.refs_0_, f32[512,256]{1,0:T(8,128)S(1)} %get-tuple-element.19.refs_1_, ...), custom_call_target="tpu_custom_call" | custom-call | tf_op jit(solution)/shard_map/write_out/pallas_call | solution.py:393

commit v5 on v4

--- a/solution.py
+++ b/solution.py
@@ -8,26 +8,26 @@
 MESH = pl.DeviceIdType.MESH
 ROWS, WIDTH = 512, 256
 STEP = 16
-PIECES_TWO = ((0, 0, 80), (1, 80, 80), (2, 160, 64), (0, 224, 96), (1, 320, 96), (2, 416, 96))
+PIECES_TWO = ((0, 0, 96), (1, 96, 96), (2, 192, 80), (0, 272, 80), (1, 352, 80), (2, 432, 80))
 PIECES_ONE = ((0, 0, 176), (0, 176, 176), (0, 352, 160))
 PLAN = (
-    (2, "a3", 0), (2, "a21", 0), (1, "a3", 0), (2, "a3", 1), (2, "a21", 1), (1, "a3", 1),
-    (2, "a3", 2), (2, "a21", 2), (1, "a3", 2), (2, "a3", 3), (2, "a3", 4), (2, "a3", 5),
-    (2, "b1", 0), (2, "a21", 3), (1, "b1", 0), (2, "b1", 1), (2, "b1", 2), (2, "a21", 4),
-    (2, "a21", 5), (2, "b0", 0), (2, "b0", 1), (1, "b1", 1), (2, "b1", 3), (2, "b1", 4),
-    (2, "b1", 5), (2, "b0", 2), (2, "c", 0), (2, "c", 1), (1, "b1", 2), (2, "c", 2),
-    (2, "b0", 3), (2, "a0", 0), (2, "b0", 4), (2, "b0", 5), (2, "a0", 1), (2, "c", 5),
-    (2, "a0", 2), (2, "a0", 3), (1, "d", 0), (2, "c", 3), (2, "c", 4), (2, "a0", 4),
-    (2, "d", 0), (2, "a0", 5), (2, "d", 1), (1, "d", 1), (2, "d", 2), (2, "d", 3),
-    (2, "d", 4), (2, "d", 5), (1, "d", 2), (2, "e", 0), (2, "e", 1), (2, "e", 2),
-    (2, "e", 3), (2, "e", 4), (1, "e", 0), (2, "e", 5), (2, "f", 0), (2, "f", 1),
-    (2, "f", 2), (2, "f", 3), (2, "f", 4), (1, "g", 0), (2, "f", 5), (1, "e", 1),
-    (2, "g", 0), (2, "g", 1), (2, "g", 2), (1, "e", 2), (1, "g", 1), (2, "g", 3),
-    (2, "g", 4), (2, "g", 5), (1, "g", 2),
+    (2, "a3", 0), (1, "a3", 0), (1, "a3", 1), (2, "a3", 1), (1, "a3", 2), (2, "a21", 0),
+    (2, "a3", 2), (2, "a21", 1), (2, "a21", 2), (2, "a3", 3), (2, "a3", 4), (2, "a3", 5),
+    (2, "a21", 3), (2, "b1", 0), (1, "b1", 0), (2, "b1", 1), (2, "a21", 4), (2, "b1", 2),
+    (2, "a21", 5), (2, "a0", 0), (2, "b0", 0), (1, "b1", 1), (2, "b1", 3), (2, "b0", 1),
+    (2, "b1", 4), (1, "b1", 2), (2, "b1", 5), (2, "c", 0), (2, "c", 1), (2, "c", 2),
+    (2, "b0", 2), (2, "a0", 1), (2, "a0", 2), (2, "b0", 3), (2, "b0", 4), (2, "b0", 5),
+    (2, "a0", 3), (2, "a0", 4), (2, "a0", 5), (1, "d", 0), (2, "c", 3), (2, "c", 4),
+    (2, "c", 5), (2, "d", 0), (2, "d", 1), (1, "d", 1), (2, "d", 2), (2, "d", 4),
+    (2, "d", 3), (2, "d", 5), (2, "e", 0), (1, "d", 2), (2, "e", 1), (2, "e", 2),
+    (2, "e", 4), (2, "e", 3), (2, "e", 5), (1, "e", 0), (2, "f", 0), (2, "f", 1),
+    (2, "f", 2), (1, "g", 0), (1, "e", 1), (2, "f", 4), (2, "f", 5), (2, "f", 3),
+    (2, "g", 0), (1, "e", 2), (2, "g", 1), (2, "g", 2), (1, "g", 1), (2, "g", 4),
+    (2, "g", 5), (2, "g", 3), (1, "g", 2),
 )
 ORDERS = ((1, 3, 4), (3, 4, 1), (4, 1, 3))
 LOADS = ((2, 0), (2, 1), (2, 2), (2, 3), (2, 4), (2, 5), (1, 0), (1, 1), (1, 2))
-FIRST_LOADS = 2
+FIRST_LOADS = 4
 KINDS = 4
 ARRIVALS = 7 * len(PIECES_TWO) + 4 * len(PIECES_ONE)
 

time: 42.1 us -> 41 us (0.974)
  Pallas kernels: 41.3 us -> 40.2 us
    pallas_call x1, Pallas kernels: 38.6 us -> 37.5 us  [body(): pl.pallas_call(kernel, out_shape=tuple((pltpu.VMEM(x.shape, x.dtype) for...]
where the time goes in v5:
time: 41 us; the launch traced here: 40.8 us
  Pallas kernels  40.2 us (98%)
  between operations  0.64 us (2%)
    pallas_call x1, Pallas kernels, body(): pl.pallas_call(kernel, out_shape=tuple((pltpu.VMEM(x.shape, x.dtype) for...  37.5 us
    pallas_call x1, Pallas kernels, body(): pl.pallas_call(write_out, out_shape=(small, small, wide, small, small, wi...  2.75 us

profile of v5, /device:TPU:1, one launch (start us, length us, event | category | flops | bytes accessed | tf_op | source)
XLA Modules:
  0.0 40.8 jit_solution(6709162445589572581)
XLA Ops:
  0.6 37.5 %outer_step.1 = (f32[512,256]{1,0:T(8,128)S(1)}, f32[512,256]{1,0:T(8,128)S(1)}, bf16[512,2048]{1,0:T(8,128)(2,1)S(1)}, f32[512,256]{1,0:T(8,128)S(1)}, f32[512,...) custom-call(f32[512,2048]{1,0:T(8,128)} %bitcast.12, f32[512,2048]{1,0:T(8,128)} %bitcast.13, f32[512,256]{1,0:T(8,128)} %bitcast.14, ...), custom_call_target="tpu_custom_call" | custom-call | tf_op jit(solution)/shard_map/outer_step/pallas_call | solution.py:366
  38.1 2.8 %write_out.1 = (f32[512,256]{1,0:T(8,128)}, f32[512,256]{1,0:T(8,128)}, bf16[512,2048]{1,0:T(8,128)(2,1)}, f32[512,256]{1,0:T(8,128)}, f32[512,256]{1,0:T(8,128)}, /*index=5*/bf16[512,2048]{1,0:T(8,128)(2,1)}) custom-call(f32[512,256]{1,0:T(8,128)S(1)} %get-tuple-element.18.refs_0_, f32[512,256]{1,0:T(8,128)S(1)} %get-tuple-element.19.refs_1_, ...), custom_call_target="tpu_custom_call" | custom-call | tf_op jit(solution)/shard_map/write_out/pallas_call | solution.py:393

commit v6 on v5

--- a/solution.py
+++ b/solution.py
@@ -9,21 +9,21 @@
 ROWS, WIDTH = 512, 256
 STEP = 16
 PIECES_TWO = ((0, 0, 96), (1, 96, 96), (2, 192, 80), (0, 272, 80), (1, 352, 80), (2, 432, 80))
-PIECES_ONE = ((0, 0, 176), (0, 176, 176), (0, 352, 160))
+PIECES_ONE = ((0, 0, 160), (0, 160, 160), (0, 320, 192))
 PLAN = (
-    (2, "a3", 0), (1, "a3", 0), (1, "a3", 1), (2, "a3", 1), (1, "a3", 2), (2, "a21", 0),
-    (2, "a3", 2), (2, "a21", 1), (2, "a21", 2), (2, "a3", 3), (2, "a3", 4), (2, "a3", 5),
+    (2, "a3", 0), (1, "a3", 0), (1, "a3", 1), (2, "a3", 1), (1, "a3", 2), (2, "a3", 2),
+    (2, "a21", 0), (2, "a21", 1), (2, "a21", 2), (2, "a3", 3), (2, "a3", 4), (2, "a3", 5),
     (2, "a21", 3), (2, "b1", 0), (1, "b1", 0), (2, "b1", 1), (2, "a21", 4), (2, "b1", 2),
-    (2, "a21", 5), (2, "a0", 0), (2, "b0", 0), (1, "b1", 1), (2, "b1", 3), (2, "b0", 1),
-    (2, "b1", 4), (1, "b1", 2), (2, "b1", 5), (2, "c", 0), (2, "c", 1), (2, "c", 2),
-    (2, "b0", 2), (2, "a0", 1), (2, "a0", 2), (2, "b0", 3), (2, "b0", 4), (2, "b0", 5),
-    (2, "a0", 3), (2, "a0", 4), (2, "a0", 5), (1, "d", 0), (2, "c", 3), (2, "c", 4),
-    (2, "c", 5), (2, "d", 0), (2, "d", 1), (1, "d", 1), (2, "d", 2), (2, "d", 4),
-    (2, "d", 3), (2, "d", 5), (2, "e", 0), (1, "d", 2), (2, "e", 1), (2, "e", 2),
-    (2, "e", 4), (2, "e", 3), (2, "e", 5), (1, "e", 0), (2, "f", 0), (2, "f", 1),
-    (2, "f", 2), (1, "g", 0), (1, "e", 1), (2, "f", 4), (2, "f", 5), (2, "f", 3),
-    (2, "g", 0), (1, "e", 2), (2, "g", 1), (2, "g", 2), (1, "g", 1), (2, "g", 4),
-    (2, "g", 5), (2, "g", 3), (1, "g", 2),
+    (2, "a21", 5), (1, "b1", 1), (2, "b0", 0), (2, "b0", 1), (2, "b0", 2), (2, "b1", 3),
+    (2, "b1", 4), (2, "b1", 5), (1, "b1", 2), (2, "c", 0), (2, "c", 1), (2, "b0", 3),
+    (2, "a0", 0), (2, "a0", 1), (2, "a0", 2), (2, "a0", 3), (2, "c", 2), (2, "b0", 4),
+    (2, "b0", 5), (2, "a0", 4), (1, "d", 0), (2, "c", 5), (2, "c", 3), (2, "c", 4),
+    (2, "a0", 5), (2, "d", 0), (1, "d", 1), (2, "d", 1), (2, "d", 2), (2, "d", 3),
+    (2, "d", 4), (2, "d", 5), (2, "e", 0), (1, "d", 2), (2, "e", 1), (2, "e", 2),
+    (2, "e", 3), (2, "e", 4), (1, "e", 0), (2, "e", 5), (2, "f", 0), (2, "f", 1),
+    (1, "e", 1), (2, "f", 2), (1, "g", 0), (2, "f", 4), (2, "f", 3), (2, "f", 5),
+    (1, "g", 1), (2, "g", 0), (1, "e", 2), (2, "g", 1), (2, "g", 2), (2, "g", 3),
+    (2, "g", 4), (2, "g", 5), (1, "g", 2),
 )
 ORDERS = ((1, 3, 4), (3, 4, 1), (4, 1, 3))
 LOADS = ((2, 0), (2, 1), (2, 2), (2, 3), (2, 4), (2, 5), (1, 0), (1, 1), (1, 2))

time: 41 us -> 41.3 us (level)
  the two profiles are of different devices: /device:TPU:1 before, /device:TPU:0 now
where the time goes in v6:
time: 41.3 us; the launch traced here: 41.1 us
  Pallas kernels  40.5 us (98%)
  between operations  0.64 us (2%)
    pallas_call x1, Pallas kernels, body(): pl.pallas_call(kernel, out_shape=tuple((pltpu.VMEM(x.shape, x.dtype) for...  37.8 us
    pallas_call x1, Pallas kernels, body(): pl.pallas_call(write_out, out_shape=(small, small, wide, small, small, wi...  2.75 us

profile of v6, /device:TPU:0, one launch (start us, length us, event | category | flops | bytes accessed | tf_op | source)
XLA Modules:
  0.0 41.1 jit_solution(1126548968734340769)
XLA Ops:
  0.6 37.8 %outer_step.1 = (f32[512,256]{1,0:T(8,128)S(1)}, f32[512,256]{1,0:T(8,128)S(1)}, bf16[512,2048]{1,0:T(8,128)(2,1)S(1)}, f32[512,256]{1,0:T(8,128)S(1)}, f32[512,...) custom-call(f32[512,2048]{1,0:T(8,128)} %bitcast.12, f32[512,2048]{1,0:T(8,128)} %bitcast.13, f32[512,256]{1,0:T(8,128)} %bitcast.14, ...), custom_call_target="tpu_custom_call" | custom-call | tf_op jit(solution)/shard_map/outer_step/pallas_call | solution.py:366
  38.4 2.8 %write_out.1 = (f32[512,256]{1,0:T(8,128)}, f32[512,256]{1,0:T(8,128)}, bf16[512,2048]{1,0:T(8,128)(2,1)}, f32[512,256]{1,0:T(8,128)}, f32[512,256]{1,0:T(8,128)}, /*index=5*/bf16[512,2048]{1,0:T(8,128)(2,1)}) custom-call(f32[512,256]{1,0:T(8,128)S(1)} %get-tuple-element.18.refs_0_, f32[512,256]{1,0:T(8,128)S(1)} %get-tuple-element.19.refs_1_, ...), custom_call_target="tpu_custom_call" | custom-call | tf_op jit(solution)/shard_map/write_out/pallas_call | solution.py:393
